TPU v7x, 128 devices: a whole 4x4x4 slice. The times are simulated.
128 devices in a mesh: dp: 4 (over x), ctx: 32 (over z, y, core).
Axes of the slice: x: 4, y: 4, z: 4, core: 2. Of those that a mesh axis runs over, the one named last changes fastest.
Arguments:
- segment_ids: int32 [32768], P(('dp', 'ctx')), parts along dimension 0, may hold values from 0 to 7, never falling along the last dimension, each value on 1 to 4096 neighbouring positions
- attn_query: bfloat16 [32768, 2048], P(('dp', 'ctx')), parts along dimension 0, may hold values from -96 to 96
- attention_keys: bfloat16 [32768, 256], P(('dp', 'ctx')), parts along dimension 0, may hold values from -8 to 8
- attention_values: bfloat16 [32768, 256], P(('dp', 'ctx')), parts along dimension 0, may hold values from -6 to 6
- attn_gate: bfloat16 [32768, 2048], P(('dp', 'ctx')), parts along dimension 0, may hold values from -8 to 8
- delta_query: bfloat16 [32768, 1024], P(('dp', 'ctx')), parts along dimension 0, may hold values from -400 to 400
- delta_key: bfloat16 [32768, 1024], P(('dp', 'ctx')), parts along dimension 0, may hold values from -400 to 400
- update_rule_payload: bfloat16 [32768, 2048], P(('dp', 'ctx')), parts along dimension 0, may hold values from -400 to 400
- delta_beta: float32 [32768, 16], P(('dp', 'ctx')), parts along dimension 0, may hold values from 0.1 to 0.9
- delta_decay: float32 [32768, 16], P(('dp', 'ctx')), parts along dimension 0, may hold values from -1 to 0
- delta_gate: bfloat16 [32768, 2048], P(('dp', 'ctx')), parts along dimension 0, may hold values from -8 to 8
- norm_gain: float32 [128], replicated, may hold values from 0.5 to 1.5
Outputs:
- attn_mixed: bfloat16 [32768, 2048], P(('dp', 'ctx')), parts along dimension 0
- delta_mixed: bfloat16 [32768, 2048], P(('dp', 'ctx')), parts along dimension 0
There are 4 independent parts, one for each index of `dp`. A program takes and returns all parts, laid end to end along the dimension named above; an argument that names none is the same for every part. Nothing has to cross between parts.
Inputs may be any that keep to these rules, and one draw needn't show every extreme that they name: `segment_ids`: segment ids never fall along the sequence; each of the 8 documents holds 1 to 4096 positions, and one holds exactly 4096.
All inputs are finite; a program needn't handle non-finite values.
Results may differ from a plain program's by a relative error of at most 0.0085.
Values may be sent and summed in bfloat16 or wider, within the bound.
A program may use at most 256 MiB of HBM per device.

v0:
```python
from functools import partial

import jax
import jax.numpy as jnp
from jax import lax
from jax.sharding import PartitionSpec as P

HEAD_WIDTH = 256
ROTARY_ENTRIES = 64
DK = 128
DV = 128
STRETCH = 128
DOCS = 8


rope_theta = 10000000.0
highest_value = lax.Precision.HIGHEST


def shifted(value, axis, steps):
    count = lax.axis_size(axis)
    initial, last = (max(0, -steps), min(count, count - steps))
    return lax.ppermute(value, axis, [(source, source + steps) for source in range(initial, last)])


def apply_rotary(field, shift_amount):
    half = ROTARY_ENTRIES // 2
    index = jnp.arange(half).astype(jnp.float32)
    freq = rope_theta ** (-2.0 * index / ROTARY_ENTRIES)
    angle = shift_amount.astype(jnp.float32)[:, None, None] * freq[None, None, :]
    angular_cos_table = jnp.cos(angle)
    sine = jnp.sin(angle)
    first = field[..., :half]
    second = field[..., half:ROTARY_ENTRIES]
    return jnp.concatenate(
        [
            first * angular_cos_table - second * sine,
            second * angular_cos_table + first * sine,
            field[..., ROTARY_ENTRIES:],
        ],
        axis=-1,
    )


def normalize(field):
    return field * lax.rsqrt(jnp.sum(field * field, axis=-1, keepdims=True) + 1e-06)


def starts_of(slot_number, first_rows):
    return jnp.max(
        jnp.where(first_rows[None, :] <= slot_number[:, None], first_rows[None, :], 0), axis=1
    )


def attend_half(
    query_vector, query_pos, query_start, key_rows, value_matrix, key_pos, recurrent_state
):
    best, total, accum = recurrent_state
    scores = jnp.einsum(
        "qngd,knd->ngqk", query_vector, key_rows, preferred_element_type=jnp.float32
    ) * HEAD_WIDTH ** (-0.5)
    allowed = (key_pos[None, :] <= query_pos[:, None]) & (key_pos[None, :] >= query_start[:, None])
    scores = jnp.where(allowed[None, None], scores, -jnp.inf)
    rising = jnp.max(scores, axis=-1)
    anchor = jnp.where(jnp.isfinite(rising), rising, 0.0)
    weights = jnp.where(allowed[None, None], jnp.exp(scores - anchor[..., None]), 0.0)
    factor = jnp.exp(best - anchor)
    accum = factor[..., None] * accum + jnp.einsum(
        "ngqk,knd->ngqd",
        weights.astype(jnp.bfloat16),
        value_matrix,
        preferred_element_type=jnp.float32,
    )
    total = factor * total + jnp.sum(weights, axis=-1)
    return (rising, total, accum)


def unchanged(recurrent_state):
    return recurrent_state


def per_device(
    segment_ids,
    attn_query,
    attention_keys,
    attention_values,
    attn_gate,
    delta_query,
    delta_key,
    update_rule_payload,
    delta_beta,
    delta_decay,
    delta_gate,
    norm_gain,
):
    ranks = lax.axis_size("ctx")
    rank = lax.axis_index("ctx")
    rows = segment_ids.shape[0]
    half = rows // 2
    documents = jnp.arange(DOCS, dtype=jnp.int32)
    counts = jnp.sum((segment_ids[:, None] == documents[None, :]).astype(jnp.int32), axis=0)
    totals = lax.psum(counts, "ctx")
    first_rows = jnp.cumsum(totals) - totals
    slot_number = rank * rows + jnp.arange(rows, dtype=jnp.int32)
    starts = starts_of(slot_number, first_rows)
    shift_amount = slot_number - starts
    heads_q = attn_query.shape[1] // HEAD_WIDTH
    heads_kv = attention_keys.shape[1] // HEAD_WIDTH
    shared_portion = heads_q // heads_kv
    query_vector = (
        apply_rotary(
            attn_query.astype(jnp.float32).reshape(rows, heads_q, HEAD_WIDTH), shift_amount
        )
        .astype(jnp.bfloat16)
        .reshape(rows, heads_q * HEAD_WIDTH)
    )
    key_rows = (
        apply_rotary(
            attention_keys.astype(jnp.float32).reshape(rows, heads_kv, HEAD_WIDTH), shift_amount
        )
        .astype(jnp.bfloat16)
        .reshape(rows, heads_kv * HEAD_WIDTH)
    )
    query_sets = query_vector.reshape(2, half, heads_kv, shared_portion, HEAD_WIDTH)
    gate_sets = attn_gate.reshape(2, half, heads_q * HEAD_WIDTH)
    pos_sets = slot_number.reshape(2, half)
    start_sets = starts.reshape(2, half)
    initial = (
        jnp.full((2, heads_kv, shared_portion, half), -jnp.inf, jnp.float32),
        jnp.zeros((2, heads_kv, shared_portion, half), jnp.float32),
        jnp.zeros((2, heads_kv, shared_portion, half, HEAD_WIDTH), jnp.float32),
    )
    start = jnp.int32(0)
    key_piece = lax.all_gather(key_rows, "ctx", axis=0, tiled=True)
    value_piece = lax.all_gather(attention_values, "ctx", axis=0, tiled=True)
    count = key_piece.shape[0]
    key_pos = jnp.arange(count, dtype=jnp.int32)
    key_piece = key_piece.reshape(count, heads_kv, HEAD_WIDTH)
    value_piece = value_piece.reshape(count, heads_kv, HEAD_WIDTH)
    bests = []
    sums = []
    accums = []
    for part in range(2):
        recurrent_state = (initial[0][part], initial[1][part], initial[2][part])
        active = (start <= jnp.max(pos_sets[part])) & (
            start + count - 1 >= jnp.min(start_sets[part])
        )
        work = partial(
            attend_half,
            query_sets[part],
            pos_sets[part],
            start_sets[part],
            key_piece,
            value_piece,
            key_pos,
        )
        recurrent_state = lax.cond(active, work, unchanged, recurrent_state)
        bests.append(recurrent_state[0])
        sums.append(recurrent_state[1])
        accums.append(recurrent_state[2])
    total = jnp.stack(sums)
    accum = jnp.stack(accums)
    mixed = accum / total[..., None]
    mixed = jnp.transpose(mixed, (0, 3, 1, 2, 4)).reshape(2, half, heads_q * HEAD_WIDTH)
    gated = (mixed * jax.nn.sigmoid(gate_sets.astype(jnp.float32))).astype(jnp.bfloat16)
    attn_mixed = gated.reshape(rows, heads_q * HEAD_WIDTH)
    heads_k = delta_query.shape[1] // DK
    heads_v = update_rule_payload.shape[1] // DV
    group = heads_v // heads_k
    unit_query = jnp.repeat(
        normalize(delta_query.astype(jnp.float32).reshape(rows, heads_k, DK)) * DK ** (-0.5),
        group,
        axis=1,
    )
    unit_key = jnp.repeat(
        normalize(delta_key.astype(jnp.float32).reshape(rows, heads_k, DK)), group, axis=1
    )
    value_rows = update_rule_payload.astype(jnp.float32).reshape(rows, heads_v, DV)
    stretches = rows // STRETCH

    def blocked(field):
        return jnp.transpose(
            field.reshape(stretches, STRETCH, heads_v, field.shape[-1]), (0, 2, 1, 3)
        )

    stretch_query = blocked(unit_query)
    stretch_key = blocked(unit_key)
    stretch_value = blocked(value_rows)
    beta = jnp.transpose(delta_beta.reshape(stretches, STRETCH, heads_v), (0, 2, 1))
    decay_log = jnp.transpose(delta_decay.reshape(stretches, STRETCH, heads_v), (0, 2, 1))
    fresh = (shift_amount == 0).astype(jnp.int32).reshape(stretches, STRETCH)
    resets = jnp.cumsum(fresh, axis=1)
    cumulative = jnp.cumsum(decay_log, axis=-1)
    steps_index = jnp.arange(STRETCH)
    inclusive = steps_index[:, None] >= steps_index[None, :]
    strict = steps_index[:, None] > steps_index[None, :]
    same = (resets[:, :, None] == resets[:, None, :]) & inclusive[None]
    span = jnp.where(
        same[:, None],
        jnp.exp(jnp.minimum(cumulative[..., :, None] - cumulative[..., None, :], 0.0)),
        0.0,
    )
    entry = jnp.where(resets == 0, 1.0, 0.0)[:, None, :] * jnp.exp(cumulative)
    gram = jnp.einsum("chtk,chsk->chts", stretch_key, stretch_key, precision=highest_value)
    system = jnp.eye(STRETCH, dtype=jnp.float32) + jnp.where(
        strict, beta[..., None] * span * gram, 0.0
    )
    right_hand = jnp.concatenate(
        [(beta * entry)[..., None] * stretch_key, beta[..., None] * stretch_value], axis=-1
    )
    solved = jax.scipy.linalg.solve_triangular(system, right_hand, lower=True, unit_diagonal=True)
    wide_keys = solved[..., :DK]
    base_values = solved[..., DK:]
    probe = (
        jnp.einsum("chtk,chsk->chts", stretch_query, stretch_key, precision=highest_value) * span
    )
    intra = jnp.einsum("chts,chsv->chtv", probe, base_values, precision=highest_value)
    reach = entry[..., None] * stretch_query - jnp.einsum(
        "chts,chsk->chtk", probe, wide_keys, precision=highest_value
    )
    weighted = span[..., -1, :][..., None] * stretch_key
    identity_map = jnp.eye(DK, dtype=jnp.float32)
    stretch_maps = entry[..., -1][..., None, None] * identity_map - jnp.einsum(
        "chsa,chsb->chab", weighted, wide_keys, precision=highest_value
    )
    stretch_adds = jnp.einsum("chsa,chsv->chav", weighted, base_values, precision=highest_value)

    def compose(carry, item):
        total_map, total_add = carry
        stretch_map, stretch_add = item
        new_map = jnp.einsum("hab,hbc->hac", stretch_map, total_map, precision=highest_value)
        new_add = (
            jnp.einsum("hab,hbv->hav", stretch_map, total_add, precision=highest_value)
            + stretch_add
        )
        return ((new_map, new_add), None)

    start_map = jnp.tile(identity_map[None], (heads_v, 1, 1))
    empty_state = jnp.zeros((heads_v, DK, DV), jnp.float32)
    (processor_layout, device_add), unused_maps = lax.scan(
        compose, (start_map, empty_state), (stretch_maps, stretch_adds)
    )

    def relay(step, recurrent_state):
        leaving = (
            jnp.einsum("hab,hbv->hav", processor_layout, recurrent_state, precision=highest_value)
            + device_add
        )
        return shifted(leaving.astype(jnp.bfloat16), "ctx", 1).astype(leaving.dtype)

    incoming = lax.fori_loop(0, ranks - 1, relay, empty_state)

    def emit(recurrent_state, item):
        stretch_map, stretch_add, reachable_rows, inside_rows = item
        mixed_output = inside_rows + jnp.einsum(
            "yul,ylf->yuf", reachable_rows, recurrent_state, precision=highest_value
        )
        following = (
            jnp.einsum("hab,hbv->hav", stretch_map, recurrent_state, precision=highest_value)
            + stretch_add
        )
        return (following, mixed_output)

    final_state, outputs = lax.scan(emit, incoming, (stretch_maps, stretch_adds, reach, intra))
    outputs = jnp.transpose(outputs, (0, 2, 1, 3)).reshape(rows, heads_v, DV)
    spread = lax.rsqrt(jnp.mean(outputs * outputs, axis=-1, keepdims=True) + 1e-06)
    gate_rows = jax.nn.silu(delta_gate.astype(jnp.float32).reshape(rows, heads_v, DV))
    delta_mixed = (
        (outputs * spread * norm_gain * gate_rows).reshape(rows, heads_v * DV).astype(jnp.bfloat16)
    )
    return (attn_mixed, delta_mixed)


def solution(mesh):
    return jax.shard_map(
        per_device,
        mesh=mesh,
        in_specs=(
            P(("dp", "ctx")),
            P(("dp", "ctx"), None),
            P(("dp", "ctx"), None),
            P(("dp", "ctx"), None),
            P(("dp", "ctx"), None),
            P(("dp", "ctx"), None),
            P(("dp", "ctx"), None),
            P(("dp", "ctx"), None),
            P(("dp", "ctx"), None),
            P(("dp", "ctx"), None),
            P(("dp", "ctx"), None),
            P(),
        ),
        out_specs=(P(("dp", "ctx"), None), P(("dp", "ctx"), None)),
        check_vma=False,
    )
```

profile of v0, /device:TPU:38, one launch (start us, length us, event | category | flops | bytes accessed | tf_op | source)
XLA Modules:
  0.0 1121.4 jit_solution(6396253176454620711)
XLA Ops:
  8.1 16.1 %psum.7 = s32[8]{0:T(128)S(1)} all-reduce(s32[8]{0:T(128)S(1)} %convert_reduce_fusion), channel_id=1, replica_groups=mesh['dp'=4,'ctx'=32] {'ctx'}, use_global_device_ids=true, to_apply=%region_2.0 | all-reduce | flops 8 | bytes 64 | tf_op jit(solution)/shard_map/psum | solution.py:102
  37.6 6.0 add_bitcast_fusion
  43.6 316.0 %custom-call.4 = f32[2,16,1,128,128]{3,4,2,1,0:T(8,128)} custom-call(f32[2,16,1,128,128]{4,3,2,1,0:T(8,128)} %add_bitcast_fusion), custom_call_target="InvertDiagBlocksLowerTriangular" | custom-call | tf_op jit(solution)/shard_map/jit(_solve_triangular)/vmap(vmap())/triangular_solve | solution.py:211
  361.2 4.5 fusion.111
  382.2 7.2 fusion.98
  389.4 6.0 multiply_subtract_fusion
  395.5 11.8 %while.40 = (s32[]{:T(128)}, f32[16,128,128]{2,1,0:T(8,128)S(1)}, f32[16,128,128]{2,1,0:T(8,128)}, f32[2,16,128,128]{3,2,1,0:T(8,128)S(1)}, f32[2,16,128,128]{3,2,1,0:T(8,128)}) while((s32[]{:T(128)}, f32[16,128,128]{2,1,0:T(8,128)S(1)}, f32[16,128,128]{2,1,0:T(8,128)}, f32[2,16,128,128]{3,2,1,0:T(8,128)S(1)}, ...), condition=%wide.region_20.21_spmd.clone.clone, body=%wide.region_19.20_spmd.clone.sunk.clone | while | flops 805830656 | bytes 15730286 | solution.py:240
  407.3 575.0 %while.41 = (s32[]{:T(128)}, f32[16,128,128]{2,1,0:T(8,128)}, f32[16,128,128]{2,1,0:T(8,128)S(1)}, f32[16,128,128]{2,1,0:T(8,128)}) while((s32[]{:T(128)}, f32[16,128,128]{2,1,0:T(8,128)}, f32[16,128,128]{2,1,0:T(8,128)S(1)}, f32[16,128,128]{2,1,0:T(8,128)}) %tuple.131), condition=%wide.region_22.23_spmd.clone.clone, body=%wide.region_21.22_spmd.clone.sunk.clone | while | flops 403701760 | bytes 7340135 | solution.py:251
  412.5 11.0 collective-permute-done
  431.0 11.0 collective-permute-done
  449.6 11.0 collective-permute-done
  468.1 11.0 collective-permute-done
  486.7 11.0 collective-permute-done
  505.3 11.0 collective-permute-done
  523.8 11.0 collective-permute-done
  542.4 11.0 collective-permute-done
  560.9 11.0 collective-permute-done
  579.5 11.0 collective-permute-done
  598.1 11.0 collective-permute-done
  616.6 11.0 collective-permute-done
  635.2 11.0 collective-permute-done
  653.7 11.0 collective-permute-done
  672.3 11.0 collective-permute-done
  690.9 11.0 collective-permute-done
  709.4 11.0 collective-permute-done
  728.0 11.0 collective-permute-done
  746.5 11.0 collective-permute-done
  765.1 11.0 collective-permute-done
  783.7 11.0 collective-permute-done
  802.2 11.0 collective-permute-done
  820.8 11.0 collective-permute-done
  839.3 11.0 collective-permute-done
  857.9 11.0 collective-permute-done
  876.5 11.0 collective-permute-done
  895.0 11.0 collective-permute-done
  913.6 11.0 collective-permute-done
  932.1 11.0 collective-permute-done
  950.7 11.0 collective-permute-done
  969.3 11.0 collective-permute-done
  982.4 15.3 %while.39 = (s32[]{:T(128)}, f32[16,128,128]{2,1,0:T(8,128)}, f32[2,16,128,128]{3,2,1,0:T(8,128)}, f32[2,16,128,128]{3,2,1,0:T(8,128)S(1)}, f32[2,16,128,128]{3,...) while((s32[]{:T(128)}, f32[16,128,128]{2,1,0:T(8,128)}, ...), condition=%wide.region_25.26_spmd.clone, body=%wide.region_24.25_spmd.sunk.clone | while | flops 805830656 | bytes 27265164 | solution.py:264
  1006.8 50.0 %conditional.3 = (f32[1,1,8,128]{3,2,1,0:T(8,128)S(1)}, f32[1,1,8,128,256]{4,3,2,1,0:T(8,128)S(1)}) conditional(s32[]{:T(128)} %convert_element_type.87, () %tuple.46, (s32[8192]{0:T(1024)S(1)}, s32[8192]{0:T(1024)S(1)}, s32[128]{0:T(128)S(1)}, s32[128]{0:T(128)S(1)}, bf16[8192,1,256]{0,2,1:T(8,128)(2,1)}, ...), branch_computations={%region_12.13_spmd, %region_13.16_spmd} | conditional | flops 8702401536 | bytes 117027856 | solution.py:157
  1010.1 15.3 %fusion.28 = (f32[8,128]{1,0:T(8,128)S(1)}, f32[8192,128,8]{1,0,2:T(8,128)}) fusion(pred[128,8192]{0,1:T(8,128)(4,1)S(1)} %compare_and_fusion.1, bf16[256,8,256]{2,0,1:T(8,128)(2,1)S(1)} %copy.101, bf16[8192,1,256]{0,2,1:T(8,128)(2,1)} %get-tuple-element.253), kind=kOutput, calls=%fused_computation.27 | convolution fusion | flops 4320132096 | bytes 39325696 | tf_op jit(solution)/shard_map/cond/branch_1_fun/qngd,knd->ngqk/dot_general | solution.py:59
  1025.5 14.7 %fusion.30 = f32[8,128]{1,0:T(8,128)S(1)} fusion(f32[8192,128,8]{1,0,2:T(8,128)} %get-tuple-element.301, f32[8,128]{1,0:T(8,128)S(1)} %get-tuple-element.299, pred[128,8192]{0,1:T(8,128)(4,1)S(1)} %compare_and_fusion.1), kind=kLoop, calls=%fused_computation.29 | loop fusion | flops 41942016 | bytes 34611200 | tf_op jit(solution)/shard_map/cond/branch_1_fun/reduce_sum | solution.py:74
  1040.2 16.4 %fusion.43 = f32[1,1,8,128,256]{4,3,2,1,0:T(8,128)S(1)} fusion(bf16[8192,1,256]{2,0,1:T(8,128)(2,1)} %get-tuple-element.115, f32[8192,128,8]{1,0,2:T(8,128)} %get-tuple-element.301, f32[8,128]{1,0:T(8,128)S(1)} %get-tuple-element.299, pred[128,8192]{0,1:T(8,128)(4,1)S(1)} %compare_and_fusion.1, f32[8,128]{1,0:T(8,128)S(1)} %get-tuple-element.298), kind=kOutput, calls=%fused_computation.38 | convolution fusion | flops 4337172480 | bytes 39854080 | tf_op jit(solution)/shard_map/cond/branch_1_fun/ngqk,knd->ngqd/dot_general | solution.py:68
  1056.9 51.7 %conditional.2 = (f32[1,1,8,128]{3,2,1,0:T(8,128)S(1)}, f32[1,1,8,128,256]{4,3,2,1,0:T(8,128)}) conditional(s32[]{:T(128)} %convert_element_type.84, () %tuple.44, (s32[8192]{0:T(1024)S(1)}, s32[8192]{0:T(1024)S(1)}, s32[128]{0:T(128)S(1)}, s32[128]{0:T(128)S(1)}, bf16[8192,1,256]{0,2,1:T(8,128)(2,1)}, /*index=5*/bf16[256,8,256]{0,2,1:T(8,128)(2,1)S(1)}, ...), branch_computations={%region_6.7_spmd, %region_7.10_spmd} | conditional | flops 8702401536 | bytes 117027856 | solution.py:157
  1061.0 15.4 %fusion = (f32[8,128]{1,0:T(8,128)S(1)}, f32[8192,128,8]{1,0,2:T(8,128)}) fusion(pred[128,8192]{0,1:T(8,128)(4,1)S(1)} %compare_and_fusion, bf16[256,8,256]{2,0,1:T(8,128)(2,1)} %copy.99, bf16[8192,1,256]{0,2,1:T(8,128)(2,1)} %get-tuple-element.246), kind=kOutput, calls=%fused_computation.2 | convolution fusion | flops 4320132096 | bytes 39325696 | tf_op jit(solution)/shard_map/cond/branch_1_fun/qngd,knd->ngqk/dot_general | solution.py:59
  1076.4 14.7 %fusion.2 = f32[8,128]{1,0:T(8,128)S(1)} fusion(f32[8192,128,8]{1,0,2:T(8,128)} %get-tuple-element.297, f32[8,128]{1,0:T(8,128)S(1)} %get-tuple-element.295, pred[128,8192]{0,1:T(8,128)(4,1)S(1)} %compare_and_fusion), kind=kLoop, calls=%fused_computation.4 | loop fusion | flops 41942016 | bytes 34611200 | tf_op jit(solution)/shard_map/cond/branch_1_fun/reduce_sum | solution.py:74
  1091.1 17.2 %fusion.15 = f32[1,1,8,128,256]{4,3,2,1,0:T(8,128)} fusion(bf16[8192,1,256]{2,0,1:T(8,128)(2,1)} %get-tuple-element.108, f32[8192,128,8]{1,0,2:T(8,128)} %get-tuple-element.297, f32[8,128]{1,0:T(8,128)S(1)} %get-tuple-element.295, pred[128,8192]{0,1:T(8,128)(4,1)S(1)} %compare_and_fusion, f32[8,128]{1,0:T(8,128)S(1)} %get-tuple-element.294), kind=kOutput, calls=%fused_computation.13 | convolution fusion | flops 4337172480 | bytes 39854080 | tf_op jit(solution)/shard_map/cond/branch_1_fun/ngqk,knd->ngqd/dot_general | solution.py:68
  (239 shorter events, 312.5 us)
Async XLA Ops:
  7.2 25.9 %copy-start = (f32[256,16]{0,1:T(8,128)S(1)}, f32[256,16]{0,1:T(8,128)}, u32[]{:S(2)}) copy-start(f32[256,16]{0,1:T(8,128)} %param.30) | copy-start | bytes 49156
  7.2 20.8 %copy-start.13 = (bf16[256,2048]{1,0:T(8,128)(2,1)S(1)}, bf16[256,2048]{1,0:T(8,128)(2,1)}, u32[]{:S(2)}) copy-start(bf16[256,2048]{1,0:T(8,128)(2,1)} %param.23) | copy-start | bytes 3145732
  7.2 999.6 %all-gather.3.cloned.1.call-start = ((), (), s32[]{:S(2)}) async-start(), calls=%async_computation | async-start | bytes 4325376 | tf_op jit(solution)/shard_map/all_gather | solution.py:134
  26.4 980.4 %all-gather.5.cloned.1.call-start = ((), (), s32[]{:S(2)}) async-start(), calls=%async_computation.1 | async-start | bytes 4325376 | tf_op jit(solution)/shard_map/all_gather | solution.py:135
  28.5 2.6 copy-start.12
  37.6 344.6 %copy-start.4 = (f32[256,8,2,128]{3,0,2,1:T(8,128)}, f32[256,8,2,128]{3,0,2,1:T(8,128)S(1)}, u32[]{:S(2)}) copy-start(f32[256,8,2,128]{3,0,2,1:T(8,128)S(1)} %broadcast_in_dim.138) | copy-start | bytes 6291460
  37.6 322.2 %copy-start.17 = (bf16[256,1024]{1,0:T(8,128)(2,1)S(1)}, bf16[256,1024]{1,0:T(8,128)(2,1)}, u32[]{:S(2)}) copy-start(bf16[256,1024]{1,0:T(8,128)(2,1)} %param.27) | copy-start | bytes 1572868
  361.2 4.5 copy-start.9
  371.1 3.5 copy-start.5
  382.2 7.2 copy-start.6
  410.5 12.9 %collective-permute-start = (bf16[16,128,128]{2,1,0:T(8,128)(2,1)}, bf16[16,128,128]{2,1,0:T(8,128)(2,1)}, u32[]{:S(2)}, u32[]{:S(2)}) collective-permute-start(bf16[16,128,128]{2,1,0:T(8,128)(2,1)} %fusion.185), channel_id=1, source_target_pairs={{0,1},{1,2},{2,3},{3,4},{4,5},{5,6},{6,7},{7,8},{8,9},{9,10},{10,1... | collective-permute-start | bytes 1572872 | tf_op jit(solution)/shard_map/while/body/eval_jaxpr/ppermute | solution.py:23
  429.1 12.9 %collective-permute-start = (bf16[16,128,128]{2,1,0:T(8,128)(2,1)}, bf16[16,128,128]{2,1,0:T(8,128)(2,1)}, u32[]{:S(2)}, u32[]{:S(2)}) collective-permute-start(bf16[16,128,128]{2,1,0:T(8,128)(2,1)} %fusion.185), channel_id=1, source_target_pairs={{0,1},{1,2},{2,3},{3,4},{4,5},{5,6},{6,7},{7,8},{8,9},{9,10},{10,1... | collective-permute-start | bytes 1572872 | tf_op jit(solution)/shard_map/while/body/eval_jaxpr/ppermute | solution.py:23
  447.7 12.9 %collective-permute-start = (bf16[16,128,128]{2,1,0:T(8,128)(2,1)}, bf16[16,128,128]{2,1,0:T(8,128)(2,1)}, u32[]{:S(2)}, u32[]{:S(2)}) collective-permute-start(bf16[16,128,128]{2,1,0:T(8,128)(2,1)} %fusion.185), channel_id=1, source_target_pairs={{0,1},{1,2},{2,3},{3,4},{4,5},{5,6},{6,7},{7,8},{8,9},{9,10},{10,1... | collective-permute-start | bytes 1572872 | tf_op jit(solution)/shard_map/while/body/eval_jaxpr/ppermute | solution.py:23
  466.2 12.9 %collective-permute-start = (bf16[16,128,128]{2,1,0:T(8,128)(2,1)}, bf16[16,128,128]{2,1,0:T(8,128)(2,1)}, u32[]{:S(2)}, u32[]{:S(2)}) collective-permute-start(bf16[16,128,128]{2,1,0:T(8,128)(2,1)} %fusion.185), channel_id=1, source_target_pairs={{0,1},{1,2},{2,3},{3,4},{4,5},{5,6},{6,7},{7,8},{8,9},{9,10},{10,1... | collective-permute-start | bytes 1572872 | tf_op jit(solution)/shard_map/while/body/eval_jaxpr/ppermute | solution.py:23
  484.8 12.9 %collective-permute-start = (bf16[16,128,128]{2,1,0:T(8,128)(2,1)}, bf16[16,128,128]{2,1,0:T(8,128)(2,1)}, u32[]{:S(2)}, u32[]{:S(2)}) collective-permute-start(bf16[16,128,128]{2,1,0:T(8,128)(2,1)} %fusion.185), channel_id=1, source_target_pairs={{0,1},{1,2},{2,3},{3,4},{4,5},{5,6},{6,7},{7,8},{8,9},{9,10},{10,1... | collective-permute-start | bytes 1572872 | tf_op jit(solution)/shard_map/while/body/eval_jaxpr/ppermute | solution.py:23
  503.3 12.9 %collective-permute-start = (bf16[16,128,128]{2,1,0:T(8,128)(2,1)}, bf16[16,128,128]{2,1,0:T(8,128)(2,1)}, u32[]{:S(2)}, u32[]{:S(2)}) collective-permute-start(bf16[16,128,128]{2,1,0:T(8,128)(2,1)} %fusion.185), channel_id=1, source_target_pairs={{0,1},{1,2},{2,3},{3,4},{4,5},{5,6},{6,7},{7,8},{8,9},{9,10},{10,1... | collective-permute-start | bytes 1572872 | tf_op jit(solution)/shard_map/while/body/eval_jaxpr/ppermute | solution.py:23
  521.9 12.9 %collective-permute-start = (bf16[16,128,128]{2,1,0:T(8,128)(2,1)}, bf16[16,128,128]{2,1,0:T(8,128)(2,1)}, u32[]{:S(2)}, u32[]{:S(2)}) collective-permute-start(bf16[16,128,128]{2,1,0:T(8,128)(2,1)} %fusion.185), channel_id=1, source_target_pairs={{0,1},{1,2},{2,3},{3,4},{4,5},{5,6},{6,7},{7,8},{8,9},{9,10},{10,1... | collective-permute-start | bytes 1572872 | tf_op jit(solution)/shard_map/while/body/eval_jaxpr/ppermute | solution.py:23
  540.5 12.9 %collective-permute-start = (bf16[16,128,128]{2,1,0:T(8,128)(2,1)}, bf16[16,128,128]{2,1,0:T(8,128)(2,1)}, u32[]{:S(2)}, u32[]{:S(2)}) collective-permute-start(bf16[16,128,128]{2,1,0:T(8,128)(2,1)} %fusion.185), channel_id=1, source_target_pairs={{0,1},{1,2},{2,3},{3,4},{4,5},{5,6},{6,7},{7,8},{8,9},{9,10},{10,1... | collective-permute-start | bytes 1572872 | tf_op jit(solution)/shard_map/while/body/eval_jaxpr/ppermute | solution.py:23
  559.0 12.9 %collective-permute-start = (bf16[16,128,128]{2,1,0:T(8,128)(2,1)}, bf16[16,128,128]{2,1,0:T(8,128)(2,1)}, u32[]{:S(2)}, u32[]{:S(2)}) collective-permute-start(bf16[16,128,128]{2,1,0:T(8,128)(2,1)} %fusion.185), channel_id=1, source_target_pairs={{0,1},{1,2},{2,3},{3,4},{4,5},{5,6},{6,7},{7,8},{8,9},{9,10},{10,1... | collective-permute-start | bytes 1572872 | tf_op jit(solution)/shard_map/while/body/eval_jaxpr/ppermute | solution.py:23
  577.6 12.9 %collective-permute-start = (bf16[16,128,128]{2,1,0:T(8,128)(2,1)}, bf16[16,128,128]{2,1,0:T(8,128)(2,1)}, u32[]{:S(2)}, u32[]{:S(2)}) collective-permute-start(bf16[16,128,128]{2,1,0:T(8,128)(2,1)} %fusion.185), channel_id=1, source_target_pairs={{0,1},{1,2},{2,3},{3,4},{4,5},{5,6},{6,7},{7,8},{8,9},{9,10},{10,1... | collective-permute-start | bytes 1572872 | tf_op jit(solution)/shard_map/while/body/eval_jaxpr/ppermute | solution.py:23
  596.1 12.9 %collective-permute-start = (bf16[16,128,128]{2,1,0:T(8,128)(2,1)}, bf16[16,128,128]{2,1,0:T(8,128)(2,1)}, u32[]{:S(2)}, u32[]{:S(2)}) collective-permute-start(bf16[16,128,128]{2,1,0:T(8,128)(2,1)} %fusion.185), channel_id=1, source_target_pairs={{0,1},{1,2},{2,3},{3,4},{4,5},{5,6},{6,7},{7,8},{8,9},{9,10},{10,1... | collective-permute-start | bytes 1572872 | tf_op jit(solution)/shard_map/while/body/eval_jaxpr/ppermute | solution.py:23
  614.7 12.9 %collective-permute-start = (bf16[16,128,128]{2,1,0:T(8,128)(2,1)}, bf16[16,128,128]{2,1,0:T(8,128)(2,1)}, u32[]{:S(2)}, u32[]{:S(2)}) collective-permute-start(bf16[16,128,128]{2,1,0:T(8,128)(2,1)} %fusion.185), channel_id=1, source_target_pairs={{0,1},{1,2},{2,3},{3,4},{4,5},{5,6},{6,7},{7,8},{8,9},{9,10},{10,1... | collective-permute-start | bytes 1572872 | tf_op jit(solution)/shard_map/while/body/eval_jaxpr/ppermute | solution.py:23
  633.3 12.9 %collective-permute-start = (bf16[16,128,128]{2,1,0:T(8,128)(2,1)}, bf16[16,128,128]{2,1,0:T(8,128)(2,1)}, u32[]{:S(2)}, u32[]{:S(2)}) collective-permute-start(bf16[16,128,128]{2,1,0:T(8,128)(2,1)} %fusion.185), channel_id=1, source_target_pairs={{0,1},{1,2},{2,3},{3,4},{4,5},{5,6},{6,7},{7,8},{8,9},{9,10},{10,1... | collective-permute-start | bytes 1572872 | tf_op jit(solution)/shard_map/while/body/eval_jaxpr/ppermute | solution.py:23
  651.8 12.9 %collective-permute-start = (bf16[16,128,128]{2,1,0:T(8,128)(2,1)}, bf16[16,128,128]{2,1,0:T(8,128)(2,1)}, u32[]{:S(2)}, u32[]{:S(2)}) collective-permute-start(bf16[16,128,128]{2,1,0:T(8,128)(2,1)} %fusion.185), channel_id=1, source_target_pairs={{0,1},{1,2},{2,3},{3,4},{4,5},{5,6},{6,7},{7,8},{8,9},{9,10},{10,1... | collective-permute-start | bytes 1572872 | tf_op jit(solution)/shard_map/while/body/eval_jaxpr/ppermute | solution.py:23
  670.4 12.9 %collective-permute-start = (bf16[16,128,128]{2,1,0:T(8,128)(2,1)}, bf16[16,128,128]{2,1,0:T(8,128)(2,1)}, u32[]{:S(2)}, u32[]{:S(2)}) collective-permute-start(bf16[16,128,128]{2,1,0:T(8,128)(2,1)} %fusion.185), channel_id=1, source_target_pairs={{0,1},{1,2},{2,3},{3,4},{4,5},{5,6},{6,7},{7,8},{8,9},{9,10},{10,1... | collective-permute-start | bytes 1572872 | tf_op jit(solution)/shard_map/while/body/eval_jaxpr/ppermute | solution.py:23
  688.9 12.9 %collective-permute-start = (bf16[16,128,128]{2,1,0:T(8,128)(2,1)}, bf16[16,128,128]{2,1,0:T(8,128)(2,1)}, u32[]{:S(2)}, u32[]{:S(2)}) collective-permute-start(bf16[16,128,128]{2,1,0:T(8,128)(2,1)} %fusion.185), channel_id=1, source_target_pairs={{0,1},{1,2},{2,3},{3,4},{4,5},{5,6},{6,7},{7,8},{8,9},{9,10},{10,1... | collective-permute-start | bytes 1572872 | tf_op jit(solution)/shard_map/while/body/eval_jaxpr/ppermute | solution.py:23
  707.5 12.9 %collective-permute-start = (bf16[16,128,128]{2,1,0:T(8,128)(2,1)}, bf16[16,128,128]{2,1,0:T(8,128)(2,1)}, u32[]{:S(2)}, u32[]{:S(2)}) collective-permute-start(bf16[16,128,128]{2,1,0:T(8,128)(2,1)} %fusion.185), channel_id=1, source_target_pairs={{0,1},{1,2},{2,3},{3,4},{4,5},{5,6},{6,7},{7,8},{8,9},{9,10},{10,1... | collective-permute-start | bytes 1572872 | tf_op jit(solution)/shard_map/while/body/eval_jaxpr/ppermute | solution.py:23
  726.1 12.9 %collective-permute-start = (bf16[16,128,128]{2,1,0:T(8,128)(2,1)}, bf16[16,128,128]{2,1,0:T(8,128)(2,1)}, u32[]{:S(2)}, u32[]{:S(2)}) collective-permute-start(bf16[16,128,128]{2,1,0:T(8,128)(2,1)} %fusion.185), channel_id=1, source_target_pairs={{0,1},{1,2},{2,3},{3,4},{4,5},{5,6},{6,7},{7,8},{8,9},{9,10},{10,1... | collective-permute-start | bytes 1572872 | tf_op jit(solution)/shard_map/while/body/eval_jaxpr/ppermute | solution.py:23
  744.6 12.9 %collective-permute-start = (bf16[16,128,128]{2,1,0:T(8,128)(2,1)}, bf16[16,128,128]{2,1,0:T(8,128)(2,1)}, u32[]{:S(2)}, u32[]{:S(2)}) collective-permute-start(bf16[16,128,128]{2,1,0:T(8,128)(2,1)} %fusion.185), channel_id=1, source_target_pairs={{0,1},{1,2},{2,3},{3,4},{4,5},{5,6},{6,7},{7,8},{8,9},{9,10},{10,1... | collective-permute-start | bytes 1572872 | tf_op jit(solution)/shard_map/while/body/eval_jaxpr/ppermute | solution.py:23
  763.2 12.9 %collective-permute-start = (bf16[16,128,128]{2,1,0:T(8,128)(2,1)}, bf16[16,128,128]{2,1,0:T(8,128)(2,1)}, u32[]{:S(2)}, u32[]{:S(2)}) collective-permute-start(bf16[16,128,128]{2,1,0:T(8,128)(2,1)} %fusion.185), channel_id=1, source_target_pairs={{0,1},{1,2},{2,3},{3,4},{4,5},{5,6},{6,7},{7,8},{8,9},{9,10},{10,1... | collective-permute-start | bytes 1572872 | tf_op jit(solution)/shard_map/while/body/eval_jaxpr/ppermute | solution.py:23
  781.7 12.9 %collective-permute-start = (bf16[16,128,128]{2,1,0:T(8,128)(2,1)}, bf16[16,128,128]{2,1,0:T(8,128)(2,1)}, u32[]{:S(2)}, u32[]{:S(2)}) collective-permute-start(bf16[16,128,128]{2,1,0:T(8,128)(2,1)} %fusion.185), channel_id=1, source_target_pairs={{0,1},{1,2},{2,3},{3,4},{4,5},{5,6},{6,7},{7,8},{8,9},{9,10},{10,1... | collective-permute-start | bytes 1572872 | tf_op jit(solution)/shard_map/while/body/eval_jaxpr/ppermute | solution.py:23
  800.3 12.9 %collective-permute-start = (bf16[16,128,128]{2,1,0:T(8,128)(2,1)}, bf16[16,128,128]{2,1,0:T(8,128)(2,1)}, u32[]{:S(2)}, u32[]{:S(2)}) collective-permute-start(bf16[16,128,128]{2,1,0:T(8,128)(2,1)} %fusion.185), channel_id=1, source_target_pairs={{0,1},{1,2},{2,3},{3,4},{4,5},{5,6},{6,7},{7,8},{8,9},{9,10},{10,1... | collective-permute-start | bytes 1572872 | tf_op jit(solution)/shard_map/while/body/eval_jaxpr/ppermute | solution.py:23
  818.9 12.9 %collective-permute-start = (bf16[16,128,128]{2,1,0:T(8,128)(2,1)}, bf16[16,128,128]{2,1,0:T(8,128)(2,1)}, u32[]{:S(2)}, u32[]{:S(2)}) collective-permute-start(bf16[16,128,128]{2,1,0:T(8,128)(2,1)} %fusion.185), channel_id=1, source_target_pairs={{0,1},{1,2},{2,3},{3,4},{4,5},{5,6},{6,7},{7,8},{8,9},{9,10},{10,1... | collective-permute-start | bytes 1572872 | tf_op jit(solution)/shard_map/while/body/eval_jaxpr/ppermute | solution.py:23
  837.4 12.9 %collective-permute-start = (bf16[16,128,128]{2,1,0:T(8,128)(2,1)}, bf16[16,128,128]{2,1,0:T(8,128)(2,1)}, u32[]{:S(2)}, u32[]{:S(2)}) collective-permute-start(bf16[16,128,128]{2,1,0:T(8,128)(2,1)} %fusion.185), channel_id=1, source_target_pairs={{0,1},{1,2},{2,3},{3,4},{4,5},{5,6},{6,7},{7,8},{8,9},{9,10},{10,1... | collective-permute-start | bytes 1572872 | tf_op jit(solution)/shard_map/while/body/eval_jaxpr/ppermute | solution.py:23
  856.0 12.9 %collective-permute-start = (bf16[16,128,128]{2,1,0:T(8,128)(2,1)}, bf16[16,128,128]{2,1,0:T(8,128)(2,1)}, u32[]{:S(2)}, u32[]{:S(2)}) collective-permute-start(bf16[16,128,128]{2,1,0:T(8,128)(2,1)} %fusion.185), channel_id=1, source_target_pairs={{0,1},{1,2},{2,3},{3,4},{4,5},{5,6},{6,7},{7,8},{8,9},{9,10},{10,1... | collective-permute-start | bytes 1572872 | tf_op jit(solution)/shard_map/while/body/eval_jaxpr/ppermute | solution.py:23
  874.5 12.9 %collective-permute-start = (bf16[16,128,128]{2,1,0:T(8,128)(2,1)}, bf16[16,128,128]{2,1,0:T(8,128)(2,1)}, u32[]{:S(2)}, u32[]{:S(2)}) collective-permute-start(bf16[16,128,128]{2,1,0:T(8,128)(2,1)} %fusion.185), channel_id=1, source_target_pairs={{0,1},{1,2},{2,3},{3,4},{4,5},{5,6},{6,7},{7,8},{8,9},{9,10},{10,1... | collective-permute-start | bytes 1572872 | tf_op jit(solution)/shard_map/while/body/eval_jaxpr/ppermute | solution.py:23
  893.1 12.9 %collective-permute-start = (bf16[16,128,128]{2,1,0:T(8,128)(2,1)}, bf16[16,128,128]{2,1,0:T(8,128)(2,1)}, u32[]{:S(2)}, u32[]{:S(2)}) collective-permute-start(bf16[16,128,128]{2,1,0:T(8,128)(2,1)} %fusion.185), channel_id=1, source_target_pairs={{0,1},{1,2},{2,3},{3,4},{4,5},{5,6},{6,7},{7,8},{8,9},{9,10},{10,1... | collective-permute-start | bytes 1572872 | tf_op jit(solution)/shard_map/while/body/eval_jaxpr/ppermute | solution.py:23
  911.7 12.9 %collective-permute-start = (bf16[16,128,128]{2,1,0:T(8,128)(2,1)}, bf16[16,128,128]{2,1,0:T(8,128)(2,1)}, u32[]{:S(2)}, u32[]{:S(2)}) collective-permute-start(bf16[16,128,128]{2,1,0:T(8,128)(2,1)} %fusion.185), channel_id=1, source_target_pairs={{0,1},{1,2},{2,3},{3,4},{4,5},{5,6},{6,7},{7,8},{8,9},{9,10},{10,1... | collective-permute-start | bytes 1572872 | tf_op jit(solution)/shard_map/while/body/eval_jaxpr/ppermute | solution.py:23
  930.2 12.9 %collective-permute-start = (bf16[16,128,128]{2,1,0:T(8,128)(2,1)}, bf16[16,128,128]{2,1,0:T(8,128)(2,1)}, u32[]{:S(2)}, u32[]{:S(2)}) collective-permute-start(bf16[16,128,128]{2,1,0:T(8,128)(2,1)} %fusion.185), channel_id=1, source_target_pairs={{0,1},{1,2},{2,3},{3,4},{4,5},{5,6},{6,7},{7,8},{8,9},{9,10},{10,1... | collective-permute-start | bytes 1572872 | tf_op jit(solution)/shard_map/while/body/eval_jaxpr/ppermute | solution.py:23
  948.8 12.9 %collective-permute-start = (bf16[16,128,128]{2,1,0:T(8,128)(2,1)}, bf16[16,128,128]{2,1,0:T(8,128)(2,1)}, u32[]{:S(2)}, u32[]{:S(2)}) collective-permute-start(bf16[16,128,128]{2,1,0:T(8,128)(2,1)} %fusion.185), channel_id=1, source_target_pairs={{0,1},{1,2},{2,3},{3,4},{4,5},{5,6},{6,7},{7,8},{8,9},{9,10},{10,1... | collective-permute-start | bytes 1572872 | tf_op jit(solution)/shard_map/while/body/eval_jaxpr/ppermute | solution.py:23
  967.3 12.9 %collective-permute-start = (bf16[16,128,128]{2,1,0:T(8,128)(2,1)}, bf16[16,128,128]{2,1,0:T(8,128)(2,1)}, u32[]{:S(2)}, u32[]{:S(2)}) collective-permute-start(bf16[16,128,128]{2,1,0:T(8,128)(2,1)} %fusion.185), channel_id=1, source_target_pairs={{0,1},{1,2},{2,3},{3,4},{4,5},{5,6},{6,7},{7,8},{8,9},{9,10},{10,1... | collective-permute-start | bytes 1572872 | tf_op jit(solution)/shard_map/while/body/eval_jaxpr/ppermute | solution.py:23
  982.4 1.9 copy-start.7
  984.3 3.6 copy-start.3
  990.0 1.9 copy-start.7
  991.9 3.6 copy-start.3
  997.6 2.5 copy-start.8
  1000.1 2.6 copy-start.10
  1112.3 1.8 copy-start.1
  (8 other events, 10.4 us)
Sparse Core Ops, SparseCore 0:
  26.6 47.1 all-gather.2
  76.0 47.0 all-gather.4
where the time goes:
time: 1130 us; the launch traced here: 1120 us
  other arithmetic  437 us (39%)
  waiting for transfers between devices  342 us (30%)
  matrix products  229 us (20%)
  starting transfers between devices  59.3 us (5%)
  local copies, waits for them, and re-layouts  19.9 us (2%)
  between operations  17.5 us (2%)
  blocking collectives  16.1 us (1%)
    ppermute x31, waiting for transfers between devices, shifted(): lax.ppermute(value, axis, [(source, source + steps) for source in range(i...  341 us
    another operation x2, other arithmetic, per_device(): jax.scipy.linalg.solve_triangular(system, right_hand, lower=True, unit_di...  316 us
    dot_general x31, matrix products, relay(): jnp.einsum('hab,hbv->hav', processor_layout, recurrent_state, precision=h...  109 us
    convert_element_type x31, other arithmetic, relay(): return shifted(leaving.astype(jnp.bfloat16), 'ctx', 1).astype(leaving.dtype)  65.7 us
    ppermute x31, starting transfers between devices, shifted(): lax.ppermute(value, axis, [(source, source + steps) for source in range(i...  59.2 us
    dot_general x2, matrix products, attend_half(): jnp.einsum('ngqk,knd->ngqd', weights.astype(jnp.bfloat16), value_matrix,...  33.7 us
    dot_general x2, matrix products, attend_half(): jnp.einsum('qngd,knd->ngqk', query_vector, key_rows, preferred_element_ty...  30.7 us
    reduce_sum x2, other arithmetic, attend_half(): total = factor * total + jnp.sum(weights, axis=-1)  29.4 us
  transfers between devices with their start and end apart: 33, of which 31 were waited for; matrix products, arithmetic and copies ran while one was open for 51% of the time, Pallas kernels for 0%

commit v1 on v0

v1 whole, which is shorter than its diff:
```python
import functools

import jax
import jax.numpy as jnp
from jax import lax
from jax.experimental import pallas as pl
from jax.experimental.pallas import tpu as pltpu
from jax.sharding import PartitionSpec as P

HEAD_WIDTH = 256
ROTARY_ENTRIES = 64
ROPE_THETA = 10000000.0
DK = 128
DOCS = 8
ROWS = 256
RANKS = 32
SLOTS = 17
HEADS_Q = 8
HEADS_K = 8
HEADS_V = 16
GROUPS = 4
PER = HEADS_K // GROUPS
MESH = pl.DeviceIdType.MESH
F32 = jnp.float32
BF16 = jnp.bfloat16
NEG = -1e30


def nn(a, b):
    return lax.dot_general(a, b, (((1,), (0,)), ((), ())), preferred_element_type=F32)


def nt(a, b):
    return lax.dot_general(a, b, (((1,), (1,)), ((), ())), preferred_element_type=F32)


def tn(a, b):
    return lax.dot_general(a, b, (((0,), (0,)), ((), ())), preferred_element_type=F32)


def iota(shape, dim):
    return lax.broadcasted_iota(jnp.int32, shape, dim)


def lanes(index, width):
    return pl.ds(pl.multiple_of(index * width, width), width)


def rotate(x, cos, sin):
    lane = iota(x.shape, 1)
    swapped = jnp.where(lane < 32, pltpu.roll(x, 96, 1), pltpu.roll(x, 32, 1))
    return x * cos + swapped * sin


def pair_diag(packed):
    zero = jnp.zeros((128, 128), packed.dtype)
    return jnp.concatenate(
        [
            jnp.concatenate([packed[:, :128], zero], axis=1),
            jnp.concatenate([zero, packed[:, 128:]], axis=1),
        ],
        axis=0,
    )


def inverse(lower):
    row = iota((128, 256), 0)
    col = iota((128, 256), 1) % 128
    apart = row ^ col
    packed = jnp.concatenate([lower[:128, :128], lower[128:, 128:]], axis=1)
    inv = jnp.where(apart == 0, 1.0, 0.0) - jnp.where(apart == 1, packed, 0.0)
    block = 2
    while block < 128:
        here = (apart >= block) & (apart < 2 * block)
        off = jnp.where(here, packed, 0.0).astype(BF16)
        inv_b = inv.astype(BF16)
        left = nn(inv_b, pair_diag(off)).astype(BF16)
        inv = inv - nn(left, pair_diag(inv_b))
        block *= 2
    inv_b = inv.astype(BF16)
    first, second = inv_b[:, :128], inv_b[:, 128:]
    corner = nn(second, nn(lower[128:, :128].astype(BF16), first).astype(BF16))
    return jnp.concatenate(
        [
            jnp.concatenate([first, jnp.zeros((128, 128), BF16)], axis=1),
            jnp.concatenate([(-corner).astype(BF16), second], axis=1),
        ],
        axis=0,
    )


def kernel(
    seg_col, seg_row, freq, q, k, v, gate, dq, dk, pv, beta, decay, dgate, gain,
    attn_out, delta_out,
    cnt, counts, kv, colg, colb, row_pack, mta, reach, intra, inbox, stage, state_in,
    qr, s_buf, tables, state,
    cnt_send, cnt_recv, kv_send, kv_recv, mta_send, mta_recv, st_send, st_recv,
):
    me = lax.axis_index("ctx")
    core = lax.rem(me, 2)
    chip = me // 2
    y = lax.rem(chip, 4)
    z = chip // 4

    def at(zz, yy, cc):
        return {"ctx": (lax.rem(zz, 4) * 4 + lax.rem(yy, 4)) * 2 + cc}

    barrier = pltpu.get_barrier_semaphore()

    @pl.loop(1, RANKS)
    def _(j):
        pl.semaphore_signal(
            barrier, inc=1, device_id={"ctx": lax.rem(me + j, RANKS)}, device_id_type=MESH
        )

    pl.semaphore_wait(barrier, RANKS - 1)

    lane1 = iota((ROWS, 128), 1)
    seg = seg_col[...]
    mine = jnp.sum(jnp.where(seg == lane1, 1.0, 0.0), axis=0, keepdims=True)
    cnt[...] = jnp.broadcast_to(mine, (8, 128))
    counts[0] = jnp.broadcast_to(mine, (8, 128))

    @pl.loop(1, RANKS)
    def _(j):
        pltpu.make_async_remote_copy(
            cnt, counts.at[j], cnt_send, cnt_recv,
            device_id={"ctx": lax.rem(me + j, RANKS)}, device_id_type=MESH,
        ).start()

    pack = jnp.zeros((ROWS, 128), F32)
    triangle = jnp.where(iota((ROWS, ROWS), 0) >= iota((ROWS, ROWS), 1), 1.0, 0.0).astype(BF16)
    dec = decay[...]
    hi = dec.astype(BF16)
    mid = (dec - hi.astype(F32)).astype(BF16)
    low = (dec - hi.astype(F32) - mid.astype(F32)).astype(BF16)
    sums = nn(triangle, hi) + nn(triangle, mid) + nn(triangle, low)
    bet = beta[...]
    for g in range(GROUPS):
        w = 2 * PER
        colg[g, :, :w] = sums[:, g * w : (g + 1) * w]
        colb[g, :, :w] = bet[:, g * w : (g + 1) * w]
    pack = jnp.concatenate([sums, jnp.zeros((ROWS, 112), F32)], axis=1)
    for h in range(HEADS_K):
        kf = dk[:, h * DK : (h + 1) * DK].astype(F32)
        rk = lax.rsqrt(jnp.sum(kf * kf, axis=1, keepdims=True) + 1e-06)
        pack = jnp.where(lane1 == 16 + h, rk, pack)
    row_pack[...] = pack.T

    pltpu.make_async_copy(counts.at[pl.ds(1, RANKS - 1)], counts.at[pl.ds(1, RANKS - 1)], cnt_recv).wait()
    totals = jnp.sum(counts[...], axis=0)[0:1]
    starts = jnp.sum(jnp.where(lane1 < seg, totals, 0.0), axis=1, keepdims=True)
    slot = (me * ROWS).astype(F32) + iota((ROWS, 1), 0).astype(F32)
    angle = (slot - starts) * freq[...]
    sign = jnp.where(lane1 < 32, -1.0, 1.0)
    cos = jnp.cos(angle)
    sin = jnp.sin(angle) * sign
    tables[0] = cos
    tables[1] = sin
    kv[0, 0, :, :128] = rotate(k[:, :128].astype(F32), cos, sin).astype(BF16)
    kv[0, 0, :, 128:] = k[:, 128:]
    kv[0, 1] = v[...]

    def send_kv(src, dst, target):
        pltpu.make_async_remote_copy(
            kv.at[src], kv.at[dst], kv_send, kv_recv.at[dst], device_id=target, device_id_type=MESH
        ).start()

    def got_kv(j):
        pltpu.make_async_copy(kv.at[j], kv.at[j], kv_recv.at[j]).wait()

    def to_twin(d):
        send_kv(2 * d, 2 * d + 1 - 2 * core, at(z, y, 1 - core))

    send_kv(0, 8, at(z + 1, y, core))
    send_kv(0, 16, at(z + 2, y, core))
    for m in range(1, 4):

        @pl.when(y + m < 4)
        def _():
            send_kv(0, 2 * m, at(z, y + m, core))

    @pl.when(core == 0)
    def _():
        to_twin(0)

    def relay_first():
        got_kv(8)
        for m in range(1, 4):
            wrap = (y + m) // 4
            send_kv(8, 2 * (4 + m - 4 * wrap), at(z, y + m, core))
        to_twin(4)

    def relay_second():
        got_kv(16)
        for m in range(1, 4):

            @pl.when(y + m >= 4)
            def _():
                send_kv(16, 2 * (m + 4), at(z, y + m, core))

        @pl.when(core == 1)
        def _():
            to_twin(8)

    def relay_third():
        for d in (1, 2, 3, 5, 6, 7):
            got_kv(2 * d)
            to_twin(d)

    def relay_last():
        for d in range(8):
            got_kv(2 * d + 1)

    for h in range(HEADS_Q):
        base = h * HEAD_WIDTH
        qr[h, :, :128] = (rotate(q[:, base : base + 128].astype(F32), cos, sin) * 1.0).astype(BF16)
        qr[h, :, 128:] = q[:, base + 128 : base + 256]

    first_doc = jnp.where(starts < (me * ROWS).astype(F32), 1.0, 0.0)
    row2 = iota((ROWS, ROWS), 0)
    col2 = iota((ROWS, ROWS), 1)
    same = (seg == seg_row[...]) & (row2 >= col2)
    seg_last = seg[ROWS - 1 : ROWS, :]
    last_doc = jnp.where(seg == seg_last, 1.0, 0.0)
    eye = jnp.where(iota((DK, DK), 0) == iota((DK, DK), 1), 1.0, 0.0)

    def group(g):
        for i in range(PER):
            kh = g * PER + i
            kr = dk[:, lanes(kh, DK)]
            qx = dq[:, lanes(kh, DK)]
            kf = kr.astype(F32)
            qf = qx.astype(F32)
            rk = lax.rsqrt(jnp.sum(kf * kf, axis=1, keepdims=True) + 1e-06)
            rq = lax.rsqrt(jnp.sum(qf * qf, axis=1, keepdims=True) + 1e-06) * DK ** (-0.5)
            rk_row = row_pack[pl.ds(16 + kh, 1), :]
            gram = nt(kr, kr) * (rk * rk_row)
            probe = nt(qx, kr) * (rq * rk_row)
            kn = kf * rk
            qn = qf * rq
            for n in range(2):
                h = 2 * kh + n
                gc = colg[g][:, 2 * i + n : 2 * i + n + 1]
                bc = colb[g][:, 2 * i + n : 2 * i + n + 1]
                gr = row_pack[pl.ds(h, 1), :]
                span = jnp.where(same, jnp.exp(jnp.minimum(gc - gr, 0.0)), 0.0)
                entry = first_doc * jnp.exp(gc)
                solved = inverse((span * gram) * bc)
                vf = pv[:, lanes(h, DK)].astype(F32)
                right = jnp.concatenate([kn * (bc * entry), vf * bc], axis=1).astype(BF16)
                wu = nn(solved, right).astype(BF16)
                inner = nn((span * probe).astype(BF16), wu)
                reach[h] = (qn * entry - inner[:, :DK]).astype(BF16)
                intra[h] = inner[:, DK:]
                tail = last_doc * jnp.exp(jnp.minimum(gc[ROWS - 1 : ROWS] - gc, 0.0))
                both = tn(wu, (kn * tail).astype(BF16))
                mt = eye * entry[ROWS - 1 : ROWS] - both[:DK]
                mta[h] = jnp.concatenate([mt, both[DK:]], axis=0).astype(BF16)

    def send_heads(g):
        @pl.loop(0, 2 * PER)
        def _(i):
            h = g * (2 * PER) + i
            owner = 2 * h

            @pl.when(me != owner)
            def _():
                pltpu.make_async_remote_copy(
                    mta.at[h], inbox.at[lax.rem(me - owner + RANKS, RANKS)], mta_send, mta_recv,
                    device_id={"ctx": owner}, device_id_type=MESH,
                ).start()

            @pl.when(me == owner)
            def _():
                inbox[0] = mta[h]

    @pl.loop(0, GROUPS)
    def _(g):
        group(g)
        send_heads(g)

        @pl.when(g == 0)
        def _():
            relay_first()

        @pl.when(g == 1)
        def _():
            relay_second()

        @pl.when(g == 3)
        def _():
            relay_third()

    relay_last()

    pos0 = iota((ROWS, ROWS), 1).astype(F32)

    def attend(h):
        qh = qr[h]
        best = None
        for j in range(SLOTS):
            s = nt(qh, kv[j, 0])
            pos = pos0 + ((me - j) * ROWS).astype(F32)
            allowed = pos >= starts
            if j == 0:
                allowed = allowed & (row2 >= col2)
            s = jnp.where(allowed, s, NEG)
            s_buf[j] = s
            m2 = jnp.maximum(s[:, :128], s[:, 128:])
            best = m2 if best is None else jnp.maximum(best, m2)
        top = jnp.max(best, axis=1, keepdims=True)
        total = None
        acc = None
        for j in range(SLOTS):
            w = jnp.exp((s_buf[j] - top) * (HEAD_WIDTH ** (-0.5)))
            t2 = w[:, :128] + w[:, 128:]
            total = t2 if total is None else total + t2
            part = nn(w.astype(BF16), kv[j, 1])
            acc = part if acc is None else acc + part
        total = jnp.sum(total, axis=1, keepdims=True)
        gt = gate[:, lanes(h, HEAD_WIDTH)].astype(F32)
        attn_out[:, lanes(h, HEAD_WIDTH)] = (acc / total * jax.nn.sigmoid(gt)).astype(BF16)

    @pl.loop(0, 4)
    def _(h):
        attend(h)

    @pl.when(core == 0)
    def _():
        pltpu.make_async_copy(
            inbox.at[pl.ds(1, RANKS - 1)], inbox.at[pl.ds(1, RANKS - 1)], mta_recv
        ).wait()

        state[...] = jnp.zeros((DK, DK), F32)

        @pl.loop(0, RANKS)
        def _(r):
            j = lax.rem(r - me + RANKS, RANKS)
            stage[j] = state[...].astype(BF16)
            state[...] = nn(stage[j], inbox[j, :DK]) + inbox[j, DK:].astype(F32)

            @pl.when(j != 0)
            def _():
                pltpu.make_async_remote_copy(
                    stage.at[j], state_in.at[chip], st_send, st_recv,
                    device_id={"ctx": r}, device_id_type=MESH,
                ).start()

            @pl.when(j == 0)
            def _():
                state_in[chip] = stage[0]

    @pl.loop(4, HEADS_Q)
    def _(h):
        attend(h)

    @pl.when(core == 0)
    def _():
        pltpu.make_async_copy(state_in.at[pl.ds(0, 15)], state_in.at[pl.ds(0, 15)], st_recv).wait()
        pltpu.make_async_copy(stage.at[pl.ds(1, 31)], stage.at[pl.ds(1, 31)], st_send).wait()
        pltpu.make_async_copy(mta.at[pl.ds(0, 15)], mta.at[pl.ds(0, 15)], mta_send).wait()

    @pl.when(core == 1)
    def _():
        pltpu.make_async_copy(state_in, state_in, st_recv).wait()
        pltpu.make_async_copy(mta, mta, mta_send).wait()

    @pl.loop(0, HEADS_V)
    def _(h):
        out = intra[h] + nt(reach[h], state_in[h])
        spread = lax.rsqrt(jnp.mean(out * out, axis=1, keepdims=True) + 1e-06)
        gt = dgate[:, lanes(h, DK)].astype(F32)
        res = out * spread * gain[...] * (gt * jax.nn.sigmoid(gt))
        delta_out[:, lanes(h, DK)] = res.astype(BF16)

    pltpu.make_async_copy(counts.at[pl.ds(1, 31)], counts.at[pl.ds(1, 31)], cnt_send).wait()

    pltpu.make_async_copy(kv.at[pl.ds(1, 16)], kv.at[pl.ds(1, 16)], kv_send).wait()


def per_device(
    segment_ids, attn_query, attention_keys, attention_values, attn_gate, delta_query, delta_key,
    update_rule_payload, delta_beta, delta_decay, delta_gate, norm_gain,
):
    half = ROTARY_ENTRIES // 2
    index = jnp.arange(half).astype(F32)
    freq = ROPE_THETA ** (-2.0 * index / ROTARY_ENTRIES)
    freq = jnp.concatenate([freq, freq, jnp.zeros((64,), F32)])[None]
    vmem = pl.BlockSpec(memory_space=pltpu.VMEM)
    dma = pltpu.SemaphoreType.DMA
    wide = jax.ShapeDtypeStruct((ROWS, 2048), BF16)
    return pl.pallas_call(
        kernel,
        out_shape=(wide, wide),
        in_specs=[vmem] * 14,
        out_specs=(vmem, vmem),
        scratch_shapes=[
            pltpu.VMEM((8, 128), F32),
            pltpu.VMEM((RANKS, 8, 128), F32),
            pltpu.VMEM((SLOTS, 2, ROWS, HEAD_WIDTH), BF16),
            pltpu.VMEM((GROUPS, ROWS, 2 * PER), F32),
            pltpu.VMEM((GROUPS, ROWS, 2 * PER), F32),
            pltpu.VMEM((128, ROWS), F32),
            pltpu.VMEM((HEADS_V, 2 * DK, DK), BF16),
            pltpu.VMEM((HEADS_V, ROWS, DK), BF16),
            pltpu.VMEM((HEADS_V, ROWS, DK), F32),
            pltpu.VMEM((RANKS, 2 * DK, DK), BF16),
            pltpu.VMEM((RANKS, DK, DK), BF16),
            pltpu.VMEM((HEADS_V, DK, DK), BF16),
            pltpu.VMEM((HEADS_Q, ROWS, HEAD_WIDTH), BF16),
            pltpu.VMEM((SLOTS, ROWS, ROWS), F32),
            pltpu.VMEM((2, ROWS, 128), F32),
            pltpu.VMEM((DK, DK), F32),
            dma, dma, dma, dma((SLOTS,)), dma, dma, dma, dma,
        ],
        compiler_params=pltpu.CompilerParams(
            collective_id=0, has_side_effects=True, vmem_limit_bytes=56 * 2**20
        ),
    )(
        segment_ids.reshape(ROWS, 1), segment_ids.reshape(1, ROWS), freq,
        attn_query, attention_keys, attention_values, attn_gate, delta_query, delta_key,
        update_rule_payload, delta_beta, delta_decay, delta_gate, norm_gain.reshape(1, DK),
    )


def solution(mesh):
    rows = P(("dp", "ctx"))
    wide = P(("dp", "ctx"), None)
    return jax.shard_map(
        per_device,
        mesh=mesh,
        in_specs=(rows,) + (wide,) * 10 + (P(),),
        out_specs=(wide, wide),
        check_vma=False,
    )
```

time: 1130 us -> 104 us (0.09)
  the two profiles are of different devices: /device:TPU:38 before, /device:TPU:0 now
where the time goes in v1:
time: 104 us; the launch traced here: 103 us
  Pallas kernels  95.7 us (92%)
  local copies, waits for them, and re-layouts  6.41 us (6%)
    pallas_call x1, Pallas kernels, per_device(): pl.pallas_call(kernel, out_shape=(wide, wide), in_specs=[vmem] * 14, out_...  95.7 us
    unnamed x10, local copies, waits for them, and re-layouts  5.6 us

profile of v1, /device:TPU:0, one launch (start us, length us, event | category | flops | bytes accessed | tf_op | source)
XLA Modules:
  0.0 103.4 jit_solution(5658978298280035541)
XLA Ops:
  0.7 0.7 maximum_bitcast_fusion.freq
  1.3 0.0 copy-start.1
  1.3 1.5 %copy.17.beta = f32[256,16]{1,0:T(8,128)} copy(f32[256,16]{0,1:T(8,128)} %param.20) | data formatting | bytes 32768 | tf_op args[8]
  2.8 0.0 copy-done.1
  2.8 0.0 copy-start.2
  2.8 0.7 copy.18.decay
  3.5 0.0 copy-done.2
  3.5 0.8 copy.16.seg_col
  4.3 95.7 %shard_map.131 = (bf16[256,2048]{1,0:T(8,128)(2,1)}, bf16[256,2048]{1,0:T(8,128)(2,1)}) custom-call(s32[256,1]{1,0:T(8,128)} %copy.16.seg_col, s32[1,256]{1,0:T(1,128)} %bitcast.5, f32[1,128]{1,0:T(1,128)} %maximum_bitcast_fusion.freq, bf16[256,2048]{1,0:T(8,128)(2,1)} %q.1, bf16[256,256]{1,0:T(8,128)(2,1)} %k.1, bf16[256,256]{1,0:T(8,128)(2,1)} %v.1, ...), custom_call_target="tpu_custom_call" | custom-call | tf_op jit(solution)/shard_map/pallas_call | solution.py:393
  100.0 0.0 copy-start
  100.1 2.4 %copy.21 = bf16[256,2048]{1,0:T(8,128)(2,1)} copy(bf16[256,2048]{1,0:T(8,128)(2,1)} %get-tuple-element.4) | data formatting | bytes 2097152
  102.4 0.0 copy-done
  102.4 1.0 copy.22
  (2 shorter events, 0.0 us)
Async XLA Ops:
  1.3 1.5 %copy-start.1 = (f32[256,16]{0,1:T(8,128)S(1)}, f32[256,16]{0,1:T(8,128)}, u32[]{:S(2)}) copy-start(f32[256,16]{0,1:T(8,128)} %param.21) | copy-start | bytes 49156
  2.8 0.8 copy-start.2
  100.0 2.4 %copy-start = (bf16[256,2048]{1,0:T(8,128)(2,1)S(1)}, bf16[256,2048]{1,0:T(8,128)(2,1)}, u32[]{:S(2)}) copy-start(bf16[256,2048]{1,0:T(8,128)(2,1)} %get-tuple-element.5) | copy-start | bytes 3145732

commit v2 on v1

v2 whole, which is shorter than its diff:
```python
import jax
import jax.numpy as jnp
import numpy as np
from jax import lax
from jax.experimental import pallas as pl
from jax.experimental.pallas import tpu as pltpu
from jax.sharding import PartitionSpec as P

HEAD_WIDTH = 256
ROTARY_ENTRIES = 64
ROPE_THETA = 10000000.0
DK = 128
DOCS = 8
ROWS = 256
RANKS = 32
SLOTS = 17
HEADS_Q = 8
HEADS_K = 8
HEADS_V = 16
GROUPS = 4
PER = HEADS_K // GROUPS
MESH = pl.DeviceIdType.MESH
F32 = jnp.float32
BF16 = jnp.bfloat16
NEG = -1e30
LOG2E = 1.4426950408889634
CHIPS = 16
KEY, VALUE = 0, 1


def nn(a, b):
    return lax.dot_general(a, b, (((1,), (0,)), ((), ())), preferred_element_type=F32)


def nt(a, b):
    return lax.dot_general(a, b, (((1,), (1,)), ((), ())), preferred_element_type=F32)


def tn(a, b):
    return lax.dot_general(a, b, (((0,), (0,)), ((), ())), preferred_element_type=F32)


def iota(shape, dim):
    return lax.broadcasted_iota(jnp.int32, shape, dim)


def lanes(index, width):
    return pl.ds(pl.multiple_of(index * width, width), width)


def rotate(x, cos, sin):
    lane = iota(x.shape, 1)
    swapped = jnp.where(lane < 32, pltpu.roll(x, 96, 1), pltpu.roll(x, 32, 1))
    return x * cos + swapped * sin


def pair_diag(packed):
    zero = jnp.zeros((128, 128), packed.dtype)
    return jnp.concatenate(
        [
            jnp.concatenate([packed[:, :128], zero], axis=1),
            jnp.concatenate([zero, packed[:, 128:]], axis=1),
        ],
        axis=0,
    )


def inverses(lowers):
    row = iota((128, 256), 0)
    col = iota((128, 256), 1) % 128
    apart = row ^ col
    packed = [jnp.concatenate([x[:128, :128], x[128:, 128:]], axis=1) for x in lowers]
    inv = [jnp.where(apart == 0, 1.0, 0.0) - jnp.where(apart == 1, x, 0.0) for x in packed]
    block = 2
    while block < 128:
        here = (apart >= block) & (apart < 2 * block)
        off = [jnp.where(here, x, 0.0).astype(BF16) for x in packed]
        inv_b = [x.astype(BF16) for x in inv]
        left = [nn(x, pair_diag(c)) for x, c in zip(inv_b, off)]
        inv = [x - nn(c.astype(BF16), pair_diag(b)) for x, c, b in zip(inv, left, inv_b)]
        block *= 2
    inv_b = [x.astype(BF16) for x in inv]
    half = [nn(x[128:, :128].astype(BF16), b[:, :128]) for x, b in zip(lowers, inv_b)]
    corner = [nn(b[:, 128:], c.astype(BF16)) for b, c in zip(inv_b, half)]
    return [
        jnp.concatenate(
            [
                jnp.concatenate([b[:, :128], jnp.zeros((128, 128), BF16)], axis=1),
                jnp.concatenate([(-c).astype(BF16), b[:, 128:]], axis=1),
            ],
            axis=0,
        )
        for b, c in zip(inv_b, corner)
    ]


def kernel(
    seg_row, freq, q, k, v, gate, dq, dk, pv, beta, decay, dgate, gain,
    attn_out, delta_out,
    cnt, counts, kv, colg, colb, row_pack, mta, reach, intra, inbox, stage, state_in,
    qr, s_even, s_odd, top_even, top_odd, bias, state, twin, comb,
    cnt_send, cnt_recv, kv_send, kv_recv, twin_send, twin_recv, comb_send, comb_recv,
    st_send, st_recv, st2_send, st2_recv,
):
    me = lax.axis_index("ctx")
    core = lax.rem(me, 2)
    chip = me // 2
    y = lax.rem(chip, 4)
    z = chip // 4

    def at(zz, yy, cc):
        return {"ctx": (lax.rem(zz, 4) * 4 + lax.rem(yy, 4)) * 2 + cc}

    barrier = pltpu.get_barrier_semaphore()

    @pl.loop(1, RANKS)
    def _(j):
        pl.semaphore_signal(
            barrier, inc=1, device_id={"ctx": lax.rem(me + j, RANKS)}, device_id_type=MESH
        )

    doc = iota((DOCS, ROWS), 0)
    mine = jnp.sum(jnp.where(seg_row[...] == doc, 1.0, 0.0), axis=1, keepdims=True)
    cnt[...] = jnp.broadcast_to(mine, (DOCS, 128))
    counts[0] = jnp.broadcast_to(mine, (DOCS, 128))
    lane1 = iota((ROWS, 128), 1)
    slot = (me * ROWS).astype(F32) + iota((ROWS, 1), 0).astype(F32)
    angle = slot * freq[...]
    cos = jnp.cos(angle)
    sin = jnp.sin(angle) * jnp.where(lane1 < 32, -1.0, 1.0)
    kv[0, KEY, :, :128] = rotate(k[:, :128].astype(F32), cos, sin).astype(BF16)
    kv[0, KEY, :, 128:] = k[:, 128:]
    kv[0, VALUE] = v[...]
    pl.semaphore_wait(barrier, RANKS - 1)

    def send_kv(part, src, dst, target):
        pltpu.make_async_remote_copy(
            kv.at[src, part], kv.at[dst, part], kv_send, kv_recv.at[dst, part],
            device_id=target, device_id_type=MESH,
        ).start()

    def got_kv(part, j):
        pltpu.make_async_copy(kv.at[j, part], kv.at[j, part], kv_recv.at[j, part]).wait()

    def to_twin(part, d):
        send_kv(part, 2 * d, 2 * d + 1 - 2 * core, at(z, y, 1 - core))

    def send_above(part):
        send_kv(part, 0, 8, at(z + 1, y, core))

    def send_own(part):
        for m in (1, 3, 2):

            @pl.when(y + m < 4)
            def _():
                send_kv(part, 0, 2 * m, at(z, y + m, core))

        @pl.when(core == 0)
        def _():
            to_twin(part, 0)

    def slot_of(source, m):
        return 2 * (4 + m - 4 * ((source + m) // 4))

    hop = (3, 1)
    behind = [lax.rem(y + 4 - t, 4) for t in hop]
    passed = [slot_of(b, t) for b, t in zip(behind, hop)]

    def relay_above(part):
        got_kv(part, 8)
        for m in (1, 3):
            send_kv(part, 8, slot_of(y, m), at(z, y + m, core))
        to_twin(part, 4)

    def relay_second(part):
        got_kv(part, 16)
        for m in (3, 1, 2):

            @pl.when(y + m >= 4)
            def _():
                send_kv(part, 16, 2 * (m + 4), at(z, y + m, core))

        @pl.when(core == 1)
        def _():
            to_twin(part, 8)

    def relay_passed(part):
        got_kv(part, passed[part])
        send_kv(part, passed[part], slot_of(behind[part], 2), at(z, y + hop[part], core))
        to_twin(part, passed[part] // 2)

    def relay_rest(part):
        for d in (1, 2, 3, 5, 6, 7):

            @pl.when(passed[part] != 2 * d)
            def _():
                got_kv(part, 2 * d)
                to_twin(part, d)

    def relay_last():
        for d in range(8):
            got_kv(KEY, 2 * d + 1)
            got_kv(VALUE, 2 * d + 1)

    @pl.loop(1, RANKS)
    def _(j):
        pltpu.make_async_remote_copy(
            cnt, counts.at[j], cnt_send, cnt_recv.at[jnp.minimum(j - 1, 1)],
            device_id={"ctx": lax.rem(me + j, RANKS)}, device_id_type=MESH,
        ).start()

    send_above(VALUE)
    send_above(KEY)
    send_own(VALUE)
    send_own(KEY)
    sums_of = jnp.where(iota((ROWS, ROWS), 0) <= iota((ROWS, ROWS), 1), 1.0, 0.0).astype(BF16)
    dec = decay[...]
    hi = dec.astype(BF16)
    mid = (dec - hi.astype(F32)).astype(BF16)
    low = (dec - hi.astype(F32) - mid.astype(F32)).astype(BF16)
    sums = nn(hi, sums_of) + nn(mid, sums_of) + nn(low, sums_of)
    row_pack[...] = sums
    seg_f = seg_row[...].astype(F32)
    pack = jnp.concatenate(
        [
            sums, beta[...],
            jnp.broadcast_to(seg_f, (96, ROWS)),
        ],
        axis=0,
    )
    columns = pack.T
    seg = columns[:, 32:33].astype(jnp.int32)
    for g in range(GROUPS):
        w = 2 * PER
        colg[g, :, :w] = columns[:, g * w : (g + 1) * w]
        colb[g, :, :w] = columns[:, 16 + g * w : 16 + (g + 1) * w]

    relay_above(VALUE)
    send_kv(VALUE, 0, 16, at(z + 2, y, core))
    send_kv(KEY, 0, 16, at(z + 2, y, core))

    for h in range(HEADS_Q):
        base = h * HEAD_WIDTH
        qr[h, :, :128] = rotate(q[:, base : base + 128].astype(F32), cos, sin).astype(BF16)
        qr[h, :, 128:] = q[:, base + 128 : base + 256]

    pltpu.make_async_copy(counts.at[1], counts.at[1], cnt_recv.at[0]).wait()
    held = jnp.where(counts[1] > 0.0, iota((DOCS, 128), 0).astype(F32), -1.0)
    held = jnp.where(me > 0, jnp.max(held, axis=0, keepdims=True), -1.0)
    first_doc = jnp.where(seg.astype(F32) == held[:, :1], 1.0, 0.0)
    row2 = iota((ROWS, ROWS), 0)
    col2 = iota((ROWS, ROWS), 1)
    same = (seg == seg_row[...]) & (row2 >= col2)
    seg_last = seg[ROWS - 1 : ROWS, :]
    last_doc = jnp.where(seg == seg_last, 1.0, 0.0)
    eye = jnp.where(iota((DK, DK), 0) == iota((DK, DK), 1), 1.0, 0.0)

    relay_above(KEY)

    def group(g):
        parts = []
        for i in range(PER):
            kh = g * PER + i
            kr = dk[:, lanes(kh, DK)]
            qx = dq[:, lanes(kh, DK)]
            kf = kr.astype(F32)
            qf = qx.astype(F32)
            rk = lax.rsqrt(jnp.sum(kf * kf, axis=1, keepdims=True) + 1e-06)
            rq = lax.rsqrt(jnp.sum(qf * qf, axis=1, keepdims=True) + 1e-06) * DK ** (-0.5)
            rk_row = jnp.broadcast_to(rk, (ROWS, 128)).T[0:1]
            gram = nt(kr, kr) * (rk * rk_row)
            probe = nt(qx, kr) * (rq * rk_row)
            for n in range(2):
                gc = colg[g][:, 2 * i + n : 2 * i + n + 1]
                bc = colb[g][:, 2 * i + n : 2 * i + n + 1]
                gr = row_pack[pl.ds(2 * kh + n, 1), :]
                span = jnp.where(same, jnp.exp(jnp.minimum(gc - gr, 0.0)), 0.0)
                parts.append((2 * kh + n, kf * rk, qf * rq, gc, bc, (span * gram) * bc, (span * probe).astype(BF16)))
        solved = inverses([p[5] for p in parts])

        @pl.when(g == 0)
        def _():
            relay_passed(VALUE)

        @pl.when(g == 1)
        def _():
            relay_passed(KEY)

        wus = []
        for (h, kn, qn, gc, bc, _, _), inv in zip(parts, solved):
            entry = first_doc * jnp.exp(gc)
            vf = pv[:, lanes(h, DK)].astype(F32)
            right = jnp.concatenate([kn * (bc * entry), vf * bc], axis=1).astype(BF16)
            wus.append(nn(inv, right).astype(BF16))
        inners = [nn(p[6], wu) for p, wu in zip(parts, wus)]
        boths = []
        for (h, kn, qn, gc, bc, _, _), wu in zip(parts, wus):
            tail = last_doc * jnp.exp(jnp.minimum(gc[ROWS - 1 : ROWS] - gc, 0.0))
            boths.append(tn(wu, (kn * tail).astype(BF16)))
        for (h, kn, qn, gc, bc, _, _), inner, both in zip(parts, inners, boths):
            entry = first_doc * jnp.exp(gc)
            reach[h] = (qn * entry - inner[:, :DK]).astype(BF16)
            intra[h] = inner[:, DK:]
            mt = eye * entry[ROWS - 1 : ROWS] - both[:DK]
            mta[h] = jnp.concatenate([mt, both[DK:]], axis=0).astype(BF16)

    heads = 2 * PER

    def send_heads(g):
        @pl.when(core == 0)
        def _():
            pltpu.make_async_remote_copy(
                mta.at[pl.ds(g * heads, heads)], twin.at[pl.ds(g * heads, heads)],
                twin_send, twin_recv.at[g],
                device_id={"ctx": me + 1}, device_id_type=MESH,
            ).start()

        @pl.when(core == 1)
        def _():
            pltpu.make_async_copy(
                twin.at[pl.ds(g * heads, heads)], twin.at[pl.ds(g * heads, heads)], twin_recv.at[g]
            ).wait()

            @pl.loop(0, heads)
            def _(i):
                h = g * heads + i
                both = nn(twin[h], mta[h, :DK])
                comb[h, :DK] = both[:DK].astype(BF16)
                comb[h, DK:] = (both[DK:] + mta[h, DK:].astype(F32)).astype(BF16)

    @pl.loop(0, GROUPS)
    def _(g):
        group(g)

        @pl.when(g == 0)
        def _():
            relay_second(VALUE)

        @pl.when(g == 1)
        def _():
            relay_second(KEY)

        @pl.when(g == 2)
        def _():
            relay_rest(VALUE)

        @pl.when(g == 3)
        def _():
            relay_rest(KEY)

        send_heads(g)

    relay_last()

    @pl.when(core == 1)
    def _():
        @pl.loop(0, HEADS_V)
        def _(i):
            h = lax.rem(chip + i, CHIPS)
            pltpu.make_async_remote_copy(
                comb.at[h], inbox.at[lax.rem(CHIPS - i, CHIPS)], comb_send, comb_recv,
                device_id={"ctx": 2 * h}, device_id_type=MESH,
            ).start()

    pltpu.make_async_copy(
        counts.at[pl.ds(2, RANKS - 2)], counts.at[pl.ds(2, RANKS - 2)], cnt_recv.at[1]
    ).wait()
    totals = jnp.sum(counts[...], axis=0)
    totals = jnp.concatenate([totals, totals], axis=1)
    start_row = jnp.sum(jnp.where(doc < seg_row[...], totals, 0.0), axis=0, keepdims=True)
    starts = jnp.broadcast_to(start_row, (128, ROWS)).T[:, :1]
    pos0 = iota((ROWS, ROWS), 1).astype(F32)
    for j in range(SLOTS):
        allowed = (pos0 + ((me - j) * ROWS).astype(F32)) >= starts
        if j == 0:
            allowed = allowed & (row2 >= col2)
        bias[j] = jnp.where(allowed, 0.0, NEG)

    def overlap(low, now, now_top, later, later_top):
        nxt = jnp.minimum(low + 1, HEADS_Q - 1)
        best = total = acc = None
        if now is not None:
            top = now_top[...]
            top = jnp.concatenate([top, top], axis=1)
        for j in range(SLOTS):
            if later is not None:
                s = nt(qr[nxt], kv[j, 0]) + bias[j]
                later[j] = s
                m2 = jnp.maximum(s[:, :128], s[:, 128:])
                best = m2 if best is None else jnp.maximum(best, m2)
            if now is not None:
                w = jnp.exp2((now[j] - top) * (LOG2E * HEAD_WIDTH ** (-0.5)))
                t2 = w[:, :128] + w[:, 128:]
                total = t2 if total is None else total + t2
                part = nn(w.astype(BF16), kv[j, 1])
                acc = part if acc is None else acc + part
        if later is not None:
            later_top[...] = jnp.broadcast_to(jnp.max(best, axis=1, keepdims=True), (ROWS, 128))
        if now is not None:
            total = jnp.sum(total, axis=1, keepdims=True)
            gt = gate[:, lanes(low, HEAD_WIDTH)].astype(F32)
            attn_out[:, lanes(low, HEAD_WIDTH)] = (
                acc * (1.0 / total) * jax.nn.sigmoid(gt)
            ).astype(BF16)

    def two_heads(i):
        overlap(2 * i, s_even, top_even, s_odd, top_odd)
        overlap(2 * i + 1, s_odd, top_odd, s_even, top_even)

    overlap(-1, None, None, s_even, top_even)

    @pl.loop(0, 4)
    def _(i):
        two_heads(i)

        @pl.when((core == 0) & (i == 2))
        def _():
            pltpu.make_async_copy(inbox, inbox, comb_recv).wait()
            state[...] = jnp.zeros((DK, DK), F32)

            @pl.loop(0, CHIPS)
            def _(c):
                j = lax.rem(c - chip + CHIPS, CHIPS)
                stage[j] = state[...].astype(BF16)
                state[...] = nn(stage[j], inbox[j, :DK]) + inbox[j, DK:].astype(F32)

                @pl.when(j != 0)
                def _():
                    pltpu.make_async_remote_copy(
                        stage.at[j], state_in.at[chip], st_send, st_recv,
                        device_id={"ctx": 2 * c}, device_id_type=MESH,
                    ).start()

                @pl.when(j == 0)
                def _():
                    state_in[chip] = stage[0]

        @pl.when((core == 0) & (i == 3))
        def _():
            pltpu.make_async_copy(state_in.at[pl.ds(0, 15)], state_in.at[pl.ds(0, 15)], st_recv).wait()
            pltpu.make_async_remote_copy(
                state_in, state_in, st2_send, st2_recv,
                device_id={"ctx": me + 1}, device_id_type=MESH,
            ).start()

    @pl.when(core == 1)
    def _():
        pltpu.make_async_copy(state_in, state_in, st2_recv).wait()

        @pl.loop(0, HEADS_V)
        def _(h):
            state_in[h] = (
                nn(state_in[h], twin[h, :DK]) + twin[h, DK:].astype(F32)
            ).astype(BF16)

        pltpu.make_async_copy(comb, comb, comb_send).wait()

    @pl.loop(0, HEADS_V // 4)
    def _(t):
        for i in range(4):
            h = 4 * t + i
            out = intra[h] + nt(reach[h], state_in[h])
            spread = lax.rsqrt(jnp.mean(out * out, axis=1, keepdims=True) + 1e-06)
            gt = dgate[:, lanes(h, DK)].astype(F32)
            res = out * spread * gain[...] * (gt * jax.nn.sigmoid(gt))
            delta_out[:, lanes(h, DK)] = res.astype(BF16)

    @pl.when(core == 0)
    def _():
        pltpu.make_async_copy(mta, mta, twin_send).wait()
        pltpu.make_async_copy(stage.at[pl.ds(1, 15)], stage.at[pl.ds(1, 15)], st_send).wait()
        pltpu.make_async_copy(state_in, state_in, st2_send).wait()

    pltpu.make_async_copy(counts.at[pl.ds(1, 31)], counts.at[pl.ds(1, 31)], cnt_send).wait()

    pltpu.make_async_copy(kv.at[pl.ds(1, 16)], kv.at[pl.ds(1, 16)], kv_send).wait()


def per_device(
    segment_ids, attn_query, attention_keys, attention_values, attn_gate, delta_query, delta_key,
    update_rule_payload, delta_beta, delta_decay, delta_gate, norm_gain,
):
    entry = np.arange(128)
    freq = np.where(
        entry < ROTARY_ENTRIES, ROPE_THETA ** (-2.0 * (entry % 32) / ROTARY_ENTRIES), 0.0
    ).astype(np.float32)[None]
    vmem = pl.BlockSpec(memory_space=pltpu.VMEM)
    dma = pltpu.SemaphoreType.DMA
    wide = jax.ShapeDtypeStruct((ROWS, 2048), BF16)
    return pl.pallas_call(
        kernel,
        out_shape=(wide, wide),
        in_specs=[vmem] * 13,
        out_specs=(vmem, vmem),
        scratch_shapes=[
            pltpu.VMEM((8, 128), F32),
            pltpu.VMEM((RANKS, 8, 128), F32),
            pltpu.VMEM((SLOTS, 2, ROWS, HEAD_WIDTH), BF16),
            pltpu.VMEM((GROUPS, ROWS, 2 * PER), F32),
            pltpu.VMEM((GROUPS, ROWS, 2 * PER), F32),
            pltpu.VMEM((HEADS_V, ROWS), F32),
            pltpu.VMEM((HEADS_V, 2 * DK, DK), BF16),
            pltpu.VMEM((HEADS_V, ROWS, DK), BF16),
            pltpu.VMEM((HEADS_V, ROWS, DK), F32),
            pltpu.VMEM((CHIPS, 2 * DK, DK), BF16),
            pltpu.VMEM((CHIPS, DK, DK), BF16),
            pltpu.VMEM((HEADS_V, DK, DK), BF16),
            pltpu.VMEM((HEADS_Q, ROWS, HEAD_WIDTH), BF16),
            pltpu.VMEM((SLOTS, ROWS, ROWS), F32),
            pltpu.VMEM((SLOTS, ROWS, ROWS), F32),
            pltpu.VMEM((ROWS, 128), F32),
            pltpu.VMEM((ROWS, 128), F32),
            pltpu.VMEM((SLOTS, ROWS, ROWS), F32),
            pltpu.VMEM((DK, DK), F32),
            pltpu.VMEM((HEADS_V, 2 * DK, DK), BF16),
            pltpu.VMEM((HEADS_V, 2 * DK, DK), BF16),
            dma, dma((2,)), dma, dma((SLOTS, 2)), dma, dma((GROUPS,)), dma, dma, dma, dma, dma, dma,
        ],
        compiler_params=pltpu.CompilerParams(
            collective_id=0, has_side_effects=True, vmem_limit_bytes=56 * 2**20
        ),
    )(
        segment_ids.reshape(1, ROWS), freq,
        attn_query, attention_keys, attention_values, attn_gate, delta_query, delta_key,
        update_rule_payload, delta_beta.T, delta_decay.T, delta_gate, norm_gain.reshape(1, DK),
    )


def solution(mesh):
    rows = P(("dp", "ctx"))
    wide = P(("dp", "ctx"), None)
    return jax.shard_map(
        per_device,
        mesh=mesh,
        in_specs=(rows,) + (wide,) * 10 + (P(),),
        out_specs=(wide, wide),
        check_vma=False,
    )
```

time: 104 us -> 76.9 us (0.74)
  the two profiles are of different devices: /device:TPU:0 before, /device:TPU:1 now
where the time goes in v2:
time: 76.9 us; the launch traced here: 76.8 us
  Pallas kernels  72.8 us (95%)
  local copies, waits for them, and re-layouts  3.37 us (4%)
    pallas_call x1, Pallas kernels, per_device(): pl.pallas_call(kernel, out_shape=(wide, wide), in_specs=[vmem] * 13, out_...  72.8 us
    unnamed x4, local copies, waits for them, and re-layouts  3.37 us

profile of v2, /device:TPU:1, one launch (start us, length us, event | category | flops | bytes accessed | tf_op | source)
XLA Modules:
  0.0 76.8 jit_solution(16161562770666775140)
XLA Ops:
  0.6 72.8 %shard_map.140 = (bf16[256,2048]{1,0:T(8,128)(2,1)}, bf16[256,2048]{1,0:T(8,128)(2,1)}) custom-call(s32[1,256]{1,0:T(1,128)} %bitcast.6, f32[1,128]{1,0:T(1,128)} %constant.2.clone.freq, bf16[256,2048]{1,0:T(8,128)(2,1)} %q.1, bf16[256,256]{1,0:T(8,128)(2,1)} %k.1, bf16[256,256]{1,0:T(8,128)(2,1)} %v.1, bf16[256,2048]{1,0:T(8,128)(2,1)} %gate.1, ...), custom_call_target="tpu_custom_call" | custom-call | tf_op jit(solution)/shard_map/pallas_call | solution.py:490
  73.4 0.0 copy-start
  73.4 2.4 %copy.17 = bf16[256,2048]{1,0:T(8,128)(2,1)} copy(bf16[256,2048]{1,0:T(8,128)(2,1)} %get-tuple-element.4) | data formatting | bytes 2097152
  75.8 0.0 copy-done
  75.8 1.0 %copy.18 = bf16[256,2048]{1,0:T(8,128)(2,1)} copy(bf16[256,2048]{1,0:T(8,128)(2,1)S(1)} %copy-done) | data formatting | bytes 2097152
Async XLA Ops:
  73.4 2.4 %copy-start = (bf16[256,2048]{1,0:T(8,128)(2,1)S(1)}, bf16[256,2048]{1,0:T(8,128)(2,1)}, u32[]{:S(2)}) copy-start(bf16[256,2048]{1,0:T(8,128)(2,1)} %get-tuple-element.5) | copy-start | bytes 3145732

commit v3 on v2

--- a/solution.py
+++ b/solution.py
@@ -95,12 +95,13 @@
 
 
 def kernel(
-    seg_row, freq, q, k, v, gate, dq, dk, pv, beta, decay, dgate, gain,
+    seg_row, freq, q_hbm, k, v, gate_hbm, dq_hbm, dk_hbm, pv_hbm, beta, decay, dgate_hbm, gain,
     attn_out, delta_out,
     cnt, counts, kv, colg, colb, row_pack, mta, reach, intra, inbox, stage, state_in,
     qr, s_even, s_odd, top_even, top_odd, bias, state, twin, comb,
     cnt_send, cnt_recv, kv_send, kv_recv, twin_send, twin_recv, comb_send, comb_recv,
     st_send, st_recv, st2_send, st2_recv,
+    q, gate, dq, dk, pv, dgate, in_sem,
 ):
     me = lax.axis_index("ctx")
     core = lax.rem(me, 2)
@@ -118,6 +119,15 @@
         pl.semaphore_signal(
             barrier, inc=1, device_id={"ctx": lax.rem(me + j, RANKS)}, device_id_type=MESH
         )
+
+    loads = [
+        pltpu.make_async_copy(src, dst, in_sem.at[n])
+        for n, (src, dst) in enumerate(
+            [(q_hbm, q), (dq_hbm, dq), (dk_hbm, dk), (pv_hbm, pv), (gate_hbm, gate), (dgate_hbm, dgate)]
+        )
+    ]
+    for load in loads:
+        load.start()
 
     doc = iota((DOCS, ROWS), 0)
     mine = jnp.sum(jnp.where(seg_row[...] == doc, 1.0, 0.0), axis=1, keepdims=True)
@@ -239,6 +249,7 @@
     send_kv(VALUE, 0, 16, at(z + 2, y, core))
     send_kv(KEY, 0, 16, at(z + 2, y, core))
 
+    loads[0].wait()
     for h in range(HEADS_Q):
         base = h * HEAD_WIDTH
         qr[h, :, :128] = rotate(q[:, base : base + 128].astype(F32), cos, sin).astype(BF16)
@@ -327,6 +338,13 @@
                 both = nn(twin[h], mta[h, :DK])
                 comb[h, :DK] = both[:DK].astype(BF16)
                 comb[h, DK:] = (both[DK:] + mta[h, DK:].astype(F32)).astype(BF16)
+                pltpu.make_async_remote_copy(
+                    comb.at[h], inbox.at[lax.rem(chip - h + CHIPS, CHIPS)], comb_send, comb_recv,
+                    device_id={"ctx": 2 * h}, device_id_type=MESH,
+                ).start()
+
+    for load in loads[1:4]:
+        load.wait()
 
     @pl.loop(0, GROUPS)
     def _(g):
@@ -351,16 +369,6 @@
         send_heads(g)
 
     relay_last()
-
-    @pl.when(core == 1)
-    def _():
-        @pl.loop(0, HEADS_V)
-        def _(i):
-            h = lax.rem(chip + i, CHIPS)
-            pltpu.make_async_remote_copy(
-                comb.at[h], inbox.at[lax.rem(CHIPS - i, CHIPS)], comb_send, comb_recv,
-                device_id={"ctx": 2 * h}, device_id_type=MESH,
-            ).start()
 
     pltpu.make_async_copy(
         counts.at[pl.ds(2, RANKS - 2)], counts.at[pl.ds(2, RANKS - 2)], cnt_recv.at[1]
@@ -408,12 +416,14 @@
         overlap(2 * i + 1, s_odd, top_odd, s_even, top_even)
 
     overlap(-1, None, None, s_even, top_even)
+    loads[4].wait()
+    loads[5].wait()
 
     @pl.loop(0, 4)
     def _(i):
         two_heads(i)
 
-        @pl.when((core == 0) & (i == 2))
+        @pl.when((core == 0) & (i == 1))
         def _():
             pltpu.make_async_copy(inbox, inbox, comb_recv).wait()
             state[...] = jnp.zeros((DK, DK), F32)
@@ -435,7 +445,7 @@
                 def _():
                     state_in[chip] = stage[0]
 
-        @pl.when((core == 0) & (i == 3))
+        @pl.when((core == 0) & (i == 2))
         def _():
             pltpu.make_async_copy(state_in.at[pl.ds(0, 15)], state_in.at[pl.ds(0, 15)], st_recv).wait()
             pltpu.make_async_remote_copy(
@@ -485,12 +495,13 @@
         entry < ROTARY_ENTRIES, ROPE_THETA ** (-2.0 * (entry % 32) / ROTARY_ENTRIES), 0.0
     ).astype(np.float32)[None]
     vmem = pl.BlockSpec(memory_space=pltpu.VMEM)
+    hbm = pl.BlockSpec(memory_space=pl.ANY)
     dma = pltpu.SemaphoreType.DMA
     wide = jax.ShapeDtypeStruct((ROWS, 2048), BF16)
     return pl.pallas_call(
         kernel,
         out_shape=(wide, wide),
-        in_specs=[vmem] * 13,
+        in_specs=[vmem, vmem, hbm, vmem, vmem, hbm, hbm, hbm, hbm, vmem, vmem, hbm, vmem],
         out_specs=(vmem, vmem),
         scratch_shapes=[
             pltpu.VMEM((8, 128), F32),
@@ -515,6 +526,13 @@
             pltpu.VMEM((HEADS_V, 2 * DK, DK), BF16),
             pltpu.VMEM((HEADS_V, 2 * DK, DK), BF16),
             dma, dma((2,)), dma, dma((SLOTS, 2)), dma, dma((GROUPS,)), dma, dma, dma, dma, dma, dma,
+            pltpu.VMEM((ROWS, 2048), BF16),
+            pltpu.VMEM((ROWS, 2048), BF16),
+            pltpu.VMEM((ROWS, 1024), BF16),
+            pltpu.VMEM((ROWS, 1024), BF16),
+            pltpu.VMEM((ROWS, 2048), BF16),
+            pltpu.VMEM((ROWS, 2048), BF16),
+            dma((6,)),
         ],
         compiler_params=pltpu.CompilerParams(
             collective_id=0, has_side_effects=True, vmem_limit_bytes=56 * 2**20

time: 76.9 us -> 71.6 us (0.931)
  the two profiles are of different devices: /device:TPU:1 before, /device:TPU:14 now
where the time goes in v3:
time: 71.6 us; the launch traced here: 70.9 us
  Pallas kernels  66.9 us (93%)
  local copies, waits for them, and re-layouts  3.37 us (5%)
    pallas_call x1, Pallas kernels, per_device(): pl.pallas_call(kernel, out_shape=(wide, wide), in_specs=[vmem, vmem, hbm,...  66.9 us
    unnamed x4, local copies, waits for them, and re-layouts  3.37 us

profile of v3, /device:TPU:14, one launch (start us, length us, event | category | flops | bytes accessed | tf_op | source)
XLA Modules:
  0.0 70.9 jit_solution(12657420046588271327)
XLA Ops:
  0.6 66.9 %shard_map.140 = (bf16[256,2048]{1,0:T(8,128)(2,1)}, bf16[256,2048]{1,0:T(8,128)(2,1)}) custom-call(s32[1,256]{1,0:T(1,128)} %bitcast.6, f32[1,128]{1,0:T(1,128)} %constant.2.clone.freq, bf16[256,2048]{1,0:T(8,128)(2,1)} %q_hbm.1, bf16[256,256]{1,0:T(8,128)(2,1)} %k.1, bf16[256,256]{1,0:T(8,128)(2,1)} %v.1, bf16[256,2048]{1,0:T(8,128)(2,1)} %gate_hbm.1, ...), custom_call_target="tpu_custom_call" | custom-call | tf_op jit(solution)/shard_map/pallas_call | solution.py:501
  67.5 0.0 copy-start
  67.5 2.4 %copy.17 = bf16[256,2048]{1,0:T(8,128)(2,1)} copy(bf16[256,2048]{1,0:T(8,128)(2,1)} %get-tuple-element.4) | data formatting | bytes 2097152
  69.9 0.0 copy-done
  69.9 1.0 %copy.18 = bf16[256,2048]{1,0:T(8,128)(2,1)} copy(bf16[256,2048]{1,0:T(8,128)(2,1)S(1)} %copy-done) | data formatting | bytes 2097152
Async XLA Ops:
  67.5 2.4 %copy-start = (bf16[256,2048]{1,0:T(8,128)(2,1)S(1)}, bf16[256,2048]{1,0:T(8,128)(2,1)}, u32[]{:S(2)}) copy-start(bf16[256,2048]{1,0:T(8,128)(2,1)} %get-tuple-element.5) | copy-start | bytes 3145732

commit v4 on v3

--- a/solution.py
+++ b/solution.py
@@ -332,12 +332,12 @@
                 twin.at[pl.ds(g * heads, heads)], twin.at[pl.ds(g * heads, heads)], twin_recv.at[g]
             ).wait()
 
-            @pl.loop(0, heads)
-            def _(i):
-                h = g * heads + i
-                both = nn(twin[h], mta[h, :DK])
+            hs = [g * heads + i for i in range(heads)]
+            pairs = [nn(twin[h], mta[h, :DK]) for h in hs]
+            for h, both in zip(hs, pairs):
                 comb[h, :DK] = both[:DK].astype(BF16)
                 comb[h, DK:] = (both[DK:] + mta[h, DK:].astype(F32)).astype(BF16)
+            for h in hs:
                 pltpu.make_async_remote_copy(
                     comb.at[h], inbox.at[lax.rem(chip - h + CHIPS, CHIPS)], comb_send, comb_recv,
                     device_id={"ctx": 2 * h}, device_id_type=MESH,
@@ -457,11 +457,12 @@
     def _():
         pltpu.make_async_copy(state_in, state_in, st2_recv).wait()
 
-        @pl.loop(0, HEADS_V)
-        def _(h):
-            state_in[h] = (
-                nn(state_in[h], twin[h, :DK]) + twin[h, DK:].astype(F32)
-            ).astype(BF16)
+        @pl.loop(0, HEADS_V // 8)
+        def _(t):
+            hs = [8 * t + i for i in range(8)]
+            moved = [nn(state_in[h], twin[h, :DK]) + twin[h, DK:].astype(F32) for h in hs]
+            for h, later in zip(hs, moved):
+                state_in[h] = later.astype(BF16)
 
         pltpu.make_async_copy(comb, comb, comb_send).wait()
 

time: 71.6 us -> 70.4 us (0.983)
  no operation moved by 1% of the time
where the time goes in v4:
time: 70.4 us; the launch traced here: 70.2 us
  Pallas kernels  66.2 us (94%)
  local copies, waits for them, and re-layouts  3.37 us (5%)
    pallas_call x1, Pallas kernels, per_device(): pl.pallas_call(kernel, out_shape=(wide, wide), in_specs=[vmem, vmem, hbm,...  66.2 us
    unnamed x4, local copies, waits for them, and re-layouts  3.37 us

profile of v4, /device:TPU:14, one launch (start us, length us, event | category | flops | bytes accessed | tf_op | source)
XLA Modules:
  0.0 70.2 jit_solution(13083623073996109775)
XLA Ops:
  0.6 66.2 %shard_map.140 = (bf16[256,2048]{1,0:T(8,128)(2,1)}, bf16[256,2048]{1,0:T(8,128)(2,1)}) custom-call(s32[1,256]{1,0:T(1,128)} %bitcast.6, f32[1,128]{1,0:T(1,128)} %constant.2.clone.freq, bf16[256,2048]{1,0:T(8,128)(2,1)} %q_hbm.1, bf16[256,256]{1,0:T(8,128)(2,1)} %k.1, bf16[256,256]{1,0:T(8,128)(2,1)} %v.1, bf16[256,2048]{1,0:T(8,128)(2,1)} %gate_hbm.1, ...), custom_call_target="tpu_custom_call" | custom-call | tf_op jit(solution)/shard_map/pallas_call | solution.py:502
  66.9 0.0 copy-start
  66.9 2.4 %copy.17 = bf16[256,2048]{1,0:T(8,128)(2,1)} copy(bf16[256,2048]{1,0:T(8,128)(2,1)} %get-tuple-element.4) | data formatting | bytes 2097152
  69.3 0.0 copy-done
  69.3 1.0 %copy.18 = bf16[256,2048]{1,0:T(8,128)(2,1)} copy(bf16[256,2048]{1,0:T(8,128)(2,1)S(1)} %copy-done) | data formatting | bytes 2097152
Async XLA Ops:
  66.9 2.4 %copy-start = (bf16[256,2048]{1,0:T(8,128)(2,1)S(1)}, bf16[256,2048]{1,0:T(8,128)(2,1)}, u32[]{:S(2)}) copy-start(bf16[256,2048]{1,0:T(8,128)(2,1)} %get-tuple-element.5) | copy-start | bytes 3145732

commit v5 on v4

--- a/solution.py
+++ b/solution.py
@@ -498,7 +498,7 @@
     vmem = pl.BlockSpec(memory_space=pltpu.VMEM)
     hbm = pl.BlockSpec(memory_space=pl.ANY)
     dma = pltpu.SemaphoreType.DMA
-    wide = jax.ShapeDtypeStruct((ROWS, 2048), BF16)
+    wide = pltpu.VMEM((ROWS, 2048), BF16)
     return pl.pallas_call(
         kernel,
         out_shape=(wide, wide),
@@ -536,7 +536,7 @@
             dma((6,)),
         ],
         compiler_params=pltpu.CompilerParams(
-            collective_id=0, has_side_effects=True, vmem_limit_bytes=56 * 2**20
+            collective_id=0, has_side_effects=True, vmem_limit_bytes=52 * 2**20
         ),
     )(
         segment_ids.reshape(1, ROWS), freq,

time: 70.4 us -> 67.6 us (0.960)
  local copies, waits for them, and re-layouts: 3.37 us -> 1.94 us
  Pallas kernels: 66.2 us -> 64.8 us
    unnamed x4 -> x2, local copies, waits for them, and re-layouts: 3.37 us -> 1.94 us
    pallas_call x1, Pallas kernels: 66.2 us -> 64.8 us  [per_device(): pl.pallas_call(kernel, out_shape=(wide, wide), in_specs=[vmem, vmem, hbm,...]
where the time goes in v5:
time: 67.6 us; the launch traced here: 67.4 us
  Pallas kernels  64.8 us (96%)
  local copies, waits for them, and re-layouts  1.94 us (3%)
    pallas_call x1, Pallas kernels, per_device(): pl.pallas_call(kernel, out_shape=(wide, wide), in_specs=[vmem, vmem, hbm,...  64.8 us
    unnamed x2, local copies, waits for them, and re-layouts  1.94 us

profile of v5, /device:TPU:14, one launch (start us, length us, event | category | flops | bytes accessed | tf_op | source)
XLA Modules:
  0.0 67.4 jit_solution(2070219618656869191)
XLA Ops:
  0.6 64.8 %shard_map.140 = (bf16[256,2048]{1,0:T(8,128)(2,1)S(1)}, bf16[256,2048]{1,0:T(8,128)(2,1)S(1)}) custom-call(s32[1,256]{1,0:T(1,128)} %bitcast.6, f32[1,128]{1,0:T(1,128)} %constant.2.clone.freq, bf16[256,2048]{1,0:T(8,128)(2,1)} %q_hbm.1, bf16[256,256]{1,0:T(8,128)(2,1)} %k.1, bf16[256,256]{1,0:T(8,128)(2,1)} %v.1, bf16[256,2048]{1,0:T(8,128)(2,1)} %gate_hbm.1, ...), custom_call_target="tpu_custom_call" | custom-call | tf_op jit(solution)/shard_map/pallas_call | solution.py:502
  65.5 1.0 %copy.17 = bf16[256,2048]{1,0:T(8,128)(2,1)} copy(bf16[256,2048]{1,0:T(8,128)(2,1)S(1)} %get-tuple-element.2) | data formatting | bytes 2097152
  66.5 1.0 %copy.18 = bf16[256,2048]{1,0:T(8,128)(2,1)} copy(bf16[256,2048]{1,0:T(8,128)(2,1)S(1)} %get-tuple-element.3) | data formatting | bytes 2097152

commit v6 on v5

--- a/solution.py
+++ b/solution.py
@@ -101,7 +101,7 @@
     qr, s_even, s_odd, top_even, top_odd, bias, state, twin, comb,
     cnt_send, cnt_recv, kv_send, kv_recv, twin_send, twin_recv, comb_send, comb_recv,
     st_send, st_recv, st2_send, st2_recv,
-    q, gate, dq, dk, pv, dgate, in_sem,
+    q, gate, dq, dk, pv, dgate, in_sem, open_attn, open_delta,
 ):
     me = lax.axis_index("ctx")
     core = lax.rem(me, 2)
@@ -368,8 +368,6 @@
 
         send_heads(g)
 
-    relay_last()
-
     pltpu.make_async_copy(
         counts.at[pl.ds(2, RANKS - 2)], counts.at[pl.ds(2, RANKS - 2)], cnt_recv.at[1]
     ).wait()
@@ -406,18 +404,26 @@
             later_top[...] = jnp.broadcast_to(jnp.max(best, axis=1, keepdims=True), (ROWS, 128))
         if now is not None:
             total = jnp.sum(total, axis=1, keepdims=True)
-            gt = gate[:, lanes(low, HEAD_WIDTH)].astype(F32)
             attn_out[:, lanes(low, HEAD_WIDTH)] = (
-                acc * (1.0 / total) * jax.nn.sigmoid(gt)
+                acc * (1.0 / total) * open_attn[low]
             ).astype(BF16)
 
     def two_heads(i):
         overlap(2 * i, s_even, top_even, s_odd, top_odd)
         overlap(2 * i + 1, s_odd, top_odd, s_even, top_even)
 
-    overlap(-1, None, None, s_even, top_even)
     loads[4].wait()
     loads[5].wait()
+
+    @pl.loop(0, HEADS_Q)
+    def _(h):
+        open_attn[h] = jax.nn.sigmoid(gate[:, lanes(h, HEAD_WIDTH)].astype(F32))
+        for i in range(2):
+            gt = dgate[:, lanes(2 * h + i, DK)].astype(F32)
+            open_delta[2 * h + i] = gain[...] * (gt * jax.nn.sigmoid(gt))
+
+    relay_last()
+    overlap(-1, None, None, s_even, top_even)
 
     @pl.loop(0, 4)
     def _(i):
@@ -433,6 +439,11 @@
                 j = lax.rem(c - chip + CHIPS, CHIPS)
                 stage[j] = state[...].astype(BF16)
                 state[...] = nn(stage[j], inbox[j, :DK]) + inbox[j, DK:].astype(F32)
+
+                pltpu.make_async_remote_copy(
+                    stage.at[j], state_in.at[chip], st2_send, st2_recv,
+                    device_id={"ctx": 2 * c + 1}, device_id_type=MESH,
+                ).start()
 
                 @pl.when(j != 0)
                 def _():
@@ -445,13 +456,9 @@
                 def _():
                     state_in[chip] = stage[0]
 
-        @pl.when((core == 0) & (i == 2))
-        def _():
-            pltpu.make_async_copy(state_in.at[pl.ds(0, 15)], state_in.at[pl.ds(0, 15)], st_recv).wait()
-            pltpu.make_async_remote_copy(
-                state_in, state_in, st2_send, st2_recv,
-                device_id={"ctx": me + 1}, device_id_type=MESH,
-            ).start()
+    @pl.when(core == 0)
+    def _():
+        pltpu.make_async_copy(state_in.at[pl.ds(0, 15)], state_in.at[pl.ds(0, 15)], st_recv).wait()
 
     @pl.when(core == 1)
     def _():
@@ -472,8 +479,7 @@
             h = 4 * t + i
             out = intra[h] + nt(reach[h], state_in[h])
             spread = lax.rsqrt(jnp.mean(out * out, axis=1, keepdims=True) + 1e-06)
-            gt = dgate[:, lanes(h, DK)].astype(F32)
-            res = out * spread * gain[...] * (gt * jax.nn.sigmoid(gt))
+            res = out * spread * open_delta[h]
             delta_out[:, lanes(h, DK)] = res.astype(BF16)
 
     @pl.when(core == 0)
@@ -534,6 +540,8 @@
             pltpu.VMEM((ROWS, 2048), BF16),
             pltpu.VMEM((ROWS, 2048), BF16),
             dma((6,)),
+            pltpu.VMEM((HEADS_Q, ROWS, HEAD_WIDTH), F32),
+            pltpu.VMEM((HEADS_V, ROWS, DK), F32),
         ],
         compiler_params=pltpu.CompilerParams(
             collective_id=0, has_side_effects=True, vmem_limit_bytes=52 * 2**20

time: 67.6 us -> 67.4 us (level)
  no operation moved by 1% of the time
where the time goes in v6:
time: 67.4 us; the launch traced here: 67.3 us
  Pallas kernels  64.7 us (96%)
  local copies, waits for them, and re-layouts  1.94 us (3%)
    pallas_call x1, Pallas kernels, per_device(): pl.pallas_call(kernel, out_shape=(wide, wide), in_specs=[vmem, vmem, hbm,...  64.7 us
    unnamed x2, local copies, waits for them, and re-layouts  1.94 us

profile of v6, /device:TPU:14, one launch (start us, length us, event | category | flops | bytes accessed | tf_op | source)
XLA Modules:
  0.0 67.3 jit_solution(4254070602109296419)
XLA Ops:
  0.6 64.7 %shard_map.140 = (bf16[256,2048]{1,0:T(8,128)(2,1)S(1)}, bf16[256,2048]{1,0:T(8,128)(2,1)S(1)}) custom-call(s32[1,256]{1,0:T(1,128)} %bitcast.6, f32[1,128]{1,0:T(1,128)} %constant.2.clone.freq, bf16[256,2048]{1,0:T(8,128)(2,1)} %q_hbm.1, bf16[256,256]{1,0:T(8,128)(2,1)} %k.1, bf16[256,256]{1,0:T(8,128)(2,1)} %v.1, bf16[256,2048]{1,0:T(8,128)(2,1)} %gate_hbm.1, ...), custom_call_target="tpu_custom_call" | custom-call | tf_op jit(solution)/shard_map/pallas_call | solution.py:508
  65.3 1.0 %copy.17 = bf16[256,2048]{1,0:T(8,128)(2,1)} copy(bf16[256,2048]{1,0:T(8,128)(2,1)S(1)} %get-tuple-element.2) | data formatting | bytes 2097152
  66.3 1.0 %copy.18 = bf16[256,2048]{1,0:T(8,128)(2,1)} copy(bf16[256,2048]{1,0:T(8,128)(2,1)S(1)} %get-tuple-element.3) | data formatting | bytes 2097152
